TPU v7x, 32 devices: a whole 2x2x4 slice. The times are simulated.
32 devices in a mesh: pts: 8 (over y, x, core), orb: 4 (over z).
Axes of the slice: x: 2, y: 2, z: 4, core: 2. Of those that a mesh axis runs over, the one named last changes fastest.
Arguments:
- amplitudes: float32 [64, 512, 512], P(None, 'orb'), may hold values from -6 to 6
- valence_points: float32 [512, 16384], P('orb', 'pts'), may hold values from -0.4 to 0.4
- conduction_points: float32 [512, 16384], P(None, 'pts'), may hold values from -0.4 to 0.4
- screened: float32 [16384, 16384], P('pts', 'orb'), may hold values from -0.0625 to 0.0625
- valence_energy: float32 [512], P('orb'), may hold values from -1.5 to -0.5
- conduction_energy: float32 [512], replicated, may hold values from 0.5 to 2.5
Outputs:
- second_step: float32 [64, 512, 512], P(None, 'orb')
All inputs are finite; a program needn't handle non-finite values.
Results may differ from a plain program's by a relative error of at most 0.000078.
Values sent between devices are 32-bit elements; how exact they have to be, the bound alone decides.
No kernel may reach another device: no remote copies, remote signals or barrier semaphores. Data moves between devices by JAX's collectives and lax.ppermute only.
A program may use at most 256 MiB of HBM per device.

v0:
```python
import jax
import jax.numpy as jnp
from jax import lax
from jax.sharding import PartitionSpec as P

center_shift = 2.5
highest = lax.Precision.HIGHEST


def encode_partial(block, valence_points, conduction_points):
    batch, vrows, cwidth = block.shape
    prod = jnp.dot(
        block.reshape(batch * vrows, cwidth),
        conduction_points,
        precision=highest,
        preferred_element_type=jnp.float32,
    )
    prod = prod.reshape(batch, vrows, conduction_points.shape[1])
    return jnp.sum(prod * valence_points[None], axis=1)


def source_points(partial_value, columns):
    summed = lax.psum(partial_value, "orb")
    encoded = lax.all_gather(summed, "pts", axis=1, tiled=True)
    return lax.dynamic_slice_in_dim(encoded, lax.axis_index("orb") * columns, columns, 1)


def kernel_partial(block, valence_points, conduction_points, screened):
    columns = screened.shape[1]
    chosen = source_points(encode_partial(block, valence_points, conduction_points), columns)
    local_terms = lax.dot_general(
        chosen,
        screened,
        (((1,), (1,)), ((), ())),
        precision=highest,
        preferred_element_type=jnp.float32,
    )
    interacted = lax.psum(local_terms, "orb")
    weighted = valence_points[None] * interacted[:, None, :]
    batch, vrows, prows = weighted.shape
    decoded = lax.dot_general(
        weighted.reshape(batch * vrows, prows),
        conduction_points,
        (((1,), (1,)), ((), ())),
        precision=highest,
        preferred_element_type=jnp.float32,
    )
    return decoded.reshape(batch, vrows, conduction_points.shape[0])


def chebyshev(block, older, factor, energy, valence_points, conduction_points, screened):
    partial_value = kernel_partial(block, valence_points, conduction_points, screened)
    share = lax.psum_scatter(partial_value, "pts", scatter_dimension=2, tiled=True)
    width = share.shape[2]
    start = lax.axis_index("pts") * width
    block_part = lax.dynamic_slice_in_dim(block, start, width, 2)
    energy_part = lax.dynamic_slice_in_dim(energy, start, width, 1)
    result = factor * (share + (energy_part - center_shift) * block_part)
    if older is not None:
        result = result - lax.dynamic_slice_in_dim(older, start, width, 2)
    return lax.all_gather(result, "pts", axis=2, tiled=True)


def body(
    amplitudes, valence_points, conduction_points, screened, valence_energy, conduction_energy
):
    energy = conduction_energy[None, :] - valence_energy[:, None]
    first_step = chebyshev(
        amplitudes, None, 0.5, energy, valence_points, conduction_points, screened
    )
    return chebyshev(
        first_step, amplitudes, 1.0, energy, valence_points, conduction_points, screened
    )


def solution(mesh):
    return jax.shard_map(
        body,
        mesh=mesh,
        in_specs=(
            P(None, "orb", None),
            P("orb", "pts"),
            P(None, "pts"),
            P("pts", "orb"),
            P("orb"),
            P(),
        ),
        out_specs=P(None, "orb", None),
        check_vma=False,
    )
```

profile of v0, /device:TPU:0, one launch (start us, length us, event | category | flops | bytes accessed | tf_op | source)
XLA Modules:
  0.0 1265.9 jit_solution(8436790769469547462)
XLA Ops:
  6.5 112.4 %multiply_reduce_fusion.1 = f32[64,2048]{1,0:T(8,128)} fusion(f32[128,2048]{1,0:T(8,128)} %param.7, f32[64,128,512]{2,1,0:T(8,128)} %param.6, f32[512,2048]{1,0:T(8,128)} %param.8), kind=kOutput, calls=%fused_computation.5 | convolution fusion | flops 103112638464 | bytes 22544384 | tf_op jit(solution)/shard_map/dot_general | solution.py:12
  119.0 41.1 %all-reduce.5.cloned.1.call-done = f32[64,2048]{1,0:T(8,128)} async-done(((f32[64,2048]{1,0:T(8,128)}), f32[64,2048]{1,0:T(8,128)}) %all-reduce.5.cloned.1.call-update) | async-done | bytes 524304 | tf_op jit(solution)/shard_map/psum | solution.py:23
  160.2 38.6 %all-gather.5.cloned.1.call-done = f32[64,16384]{1,0:T(8,128)} async-done(((f32[64,2048]{1,0:T(8,128)}), f32[64,16384]{1,0:T(8,128)}) %all-gather.5.cloned.1.call-update) | async-done | bytes 4194320 | tf_op jit(solution)/shard_map/all_gather | solution.py:24
  198.7 36.6 %fusion.14 = f32[64,2048]{1,0:T(8,128)} fusion(f32[2048,4096]{1,0:T(8,128)} %param.9, f32[64,16384]{1,0:T(8,128)} %all-gather.5.cloned.1.call-done, s32[]{:T(128)S(6)} %select_n.4), kind=kOutput, calls=%fused_computation.18 | convolution fusion | flops 6442450944 | bytes 35127300 | tf_op jit(solution)/shard_map/dot_general | solution.py:31
  235.4 38.4 %all-reduce.7.cloned.1.call-done = f32[64,2048]{1,0:T(8,128)} async-done(((f32[64,2048]{1,0:T(8,128)}), f32[64,2048]{1,0:T(8,128)}) %all-reduce.7.cloned.1.call-update) | async-done | bytes 524304 | tf_op jit(solution)/shard_map/psum | solution.py:38
  273.9 22.2 %fusion.27 = f32[64,128,2048]{2,1,0:T(8,128)} fusion(f32[64,2048]{1,0:T(8,128)} %all-reduce.7.cloned.1.call-done, f32[128,2048]{1,0:T(8,128)S(1)} %copy-done), kind=kLoop, calls=%fused_computation.4.clone | loop fusion | flops 16777216 | bytes 68681728 | tf_op jit(solution)/shard_map/dot_general | solution.py:41
  296.1 114.7 %fusion.2 = f32[64,128,512]{1,2,0:T(8,128)} fusion(f32[512,2048]{1,0:T(8,128)S(1)} %copy-done.2, f32[64,128,2048]{2,1,0:T(8,128)} %fusion.27), kind=kOutput, calls=%fused_computation.3 | convolution fusion | flops 103079215104 | bytes 88080384 | tf_op jit(solution)/shard_map/dot_general | solution.py:41
  410.8 0.8 dynamic-slice
  411.6 5.4 constant_dynamic-slice_fusion
  417.0 3.2 copy.9
  420.3 106.6 %reduce-scatter.3.cloned.1.call-done = f32[64,128,64]{1,2,0:T(8,128)} async-done(((f32[64,128,512]{1,2,0:T(8,128)}), f32[64,128,64]{1,2,0:T(8,128)}) %reduce-scatter.3.cloned.1.call-update) | async-done | bytes 2097168 | tf_op jit(solution)/shard_map/reduce_scatter | solution.py:53
  526.9 3.4 add_multiply_fusion
  530.4 89.9 %all-gather.7.cloned.1.call-done = f32[64,128,512]{1,2,0:T(8,128)} async-done(((f32[64,128,64]{1,2,0:T(8,128)}), f32[64,128,512]{1,2,0:T(8,128)}) %all-gather.7.cloned.1.call-update) | async-done | bytes 16777232 | tf_op jit(solution)/shard_map/all_gather | solution.py:61
  620.3 121.4 %multiply_reduce_fusion = f32[64,2048]{1,0:T(8,128)} fusion(f32[128,2048]{1,0:T(8,128)S(1)} %copy-done, f32[64,128,512]{1,2,0:T(8,128)} %all-gather.7.cloned.1.call-done, f32[512,2048]{1,0:T(8,128)} %param.8), kind=kOutput, calls=%fused_computation.2 | convolution fusion | flops 103112638464 | bytes 22544384 | tf_op jit(solution)/shard_map/dot_general | solution.py:12
  741.8 38.4 %all-reduce.9.cloned.1.call-done = f32[64,2048]{1,0:T(8,128)} async-done(((f32[64,2048]{1,0:T(8,128)}), f32[64,2048]{1,0:T(8,128)}) %all-reduce.9.cloned.1.call-update) | async-done | bytes 524304 | tf_op jit(solution)/shard_map/psum | solution.py:23
  780.3 38.6 %all-gather.9.cloned.1.call-done = f32[64,16384]{1,0:T(8,128)} async-done(((f32[64,2048]{1,0:T(8,128)}), f32[64,16384]{1,0:T(8,128)}) %all-gather.9.cloned.1.call-update) | async-done | bytes 4194320 | tf_op jit(solution)/shard_map/all_gather | solution.py:24
  818.8 36.6 %fusion.12 = f32[64,2048]{1,0:T(8,128)} fusion(f32[2048,4096]{1,0:T(8,128)} %param.9, f32[64,16384]{1,0:T(8,128)} %all-gather.9.cloned.1.call-done, s32[]{:T(128)S(6)} %select_n.4), kind=kOutput, calls=%fused_computation.16 | convolution fusion | flops 6442450944 | bytes 35127300 | tf_op jit(solution)/shard_map/dot_general | solution.py:31
  855.6 38.4 %all-reduce.11.cloned.1.call-done = f32[64,2048]{1,0:T(8,128)} async-done(((f32[64,2048]{1,0:T(8,128)}), f32[64,2048]{1,0:T(8,128)}) %all-reduce.11.cloned.1.call-update) | async-done | bytes 524304 | tf_op jit(solution)/shard_map/psum | solution.py:38
  894.0 22.2 %fusion.25 = f32[64,128,2048]{2,1,0:T(8,128)} fusion(f32[64,2048]{1,0:T(8,128)} %all-reduce.11.cloned.1.call-done, f32[128,2048]{1,0:T(8,128)S(1)} %copy-done), kind=kLoop, calls=%fused_computation.1.clone.1 | loop fusion | flops 16777216 | bytes 68681728 | tf_op jit(solution)/shard_map/dot_general | solution.py:41
  916.2 114.7 %fusion = f32[64,128,512]{1,2,0:T(8,128)} fusion(f32[512,2048]{1,0:T(8,128)S(1)} %copy-done.3, f32[64,128,2048]{2,1,0:T(8,128)} %fusion.25), kind=kOutput, calls=%fused_computation | convolution fusion | flops 103079215104 | bytes 88080384 | tf_op jit(solution)/shard_map/dot_general | solution.py:41
  1031.0 116.1 %reduce-scatter.5.cloned.1.call-done = f32[64,128,64]{1,2,0:T(8,128)} async-done(((f32[64,128,512]{1,2,0:T(8,128)}), f32[64,128,64]{1,2,0:T(8,128)}) %reduce-scatter.5.cloned.1.call-update) | async-done | bytes 2097168 | tf_op jit(solution)/shard_map/reduce_scatter | solution.py:53
  1147.0 4.2 add_subtract_fusion
  1151.3 90.0 %all-gather.11.cloned.1.call-done = f32[64,128,512]{1,2,0:T(8,128)} async-done(((f32[64,128,64]{1,2,0:T(8,128)}), f32[64,128,512]{1,2,0:T(8,128)}) %all-gather.11.cloned.1.call-update) | async-done | bytes 16777232 | tf_op jit(solution)/shard_map/all_gather | solution.py:61
  1241.3 17.4 %copy.8 = f32[64,128,512]{2,1,0:T(8,128)} copy(f32[64,128,512]{1,2,0:T(8,128)} %all-gather.11.cloned.1.call-done) | data formatting | bytes 33554432 | tf_op jit(solution)/shard_map/all_gather | solution.py:61
  (29 shorter events, 0.6 us)
Async XLA Ops:
  6.5 153.5 %all-reduce.5.cloned.1.call-start = ((), (), s32[]{:S(2)}) async-start(), calls=%async_computation.2 | async-start | bytes 1048576 | tf_op jit(solution)/shard_map/psum | solution.py:23
  119.0 79.8 %all-gather.5.cloned.1.call-start = ((), (), s32[]{:S(2)}) async-start(), calls=%async_computation.3 | async-start | bytes 4718592 | tf_op jit(solution)/shard_map/all_gather | solution.py:24
  160.1 113.7 %all-reduce.7.cloned.1.call-start = ((), (), s32[]{:S(2)}) async-start(), calls=%async_computation.4 | async-start | bytes 1048576 | tf_op jit(solution)/shard_map/psum | solution.py:38
  160.2 113.7 %copy-start = (f32[128,2048]{1,0:T(8,128)S(1)}, f32[128,2048]{1,0:T(8,128)}, u32[]{:S(2)}) copy-start(f32[128,2048]{1,0:T(8,128)} %param.7) | copy-start | bytes 3145732
  235.4 291.5 %reduce-scatter.3.cloned.1.call-start = ((), (), s32[]{:S(2)}) async-start(), calls=%async_computation.5 | async-start | bytes 18874368 | tf_op jit(solution)/shard_map/reduce_scatter | solution.py:53
  273.9 22.2 %copy-start.2 = (f32[512,2048]{1,0:T(8,128)S(1)}, f32[512,2048]{1,0:T(8,128)}, u32[]{:S(2)}) copy-start(f32[512,2048]{1,0:T(8,128)} %param.8) | copy-start | bytes 12582916
  410.8 9.5 copy-start.1
  410.8 209.5 %all-gather.7.cloned.1.call-start = ((), (), s32[]{:S(2)}) async-start(), calls=%async_computation.6 | async-start | bytes 18874368 | tf_op jit(solution)/shard_map/all_gather | solution.py:61
  530.3 249.9 %all-reduce.9.cloned.1.call-start = ((), (), s32[]{:S(2)}) async-start(), calls=%async_computation.7 | async-start | bytes 1048576 | tf_op jit(solution)/shard_map/psum | solution.py:23
  741.8 77.1 %all-gather.9.cloned.1.call-start = ((), (), s32[]{:S(2)}) async-start(), calls=%async_computation.8 | async-start | bytes 4718592 | tf_op jit(solution)/shard_map/all_gather | solution.py:24
  780.2 113.7 %all-reduce.11.cloned.1.call-start = ((), (), s32[]{:S(2)}) async-start(), calls=%async_computation.9 | async-start | bytes 1048576 | tf_op jit(solution)/shard_map/psum | solution.py:38
  855.5 291.5 %reduce-scatter.5.cloned.1.call-start = ((), (), s32[]{:S(2)}) async-start(), calls=%async_computation.10 | async-start | bytes 18874368 | tf_op jit(solution)/shard_map/reduce_scatter | solution.py:53
  894.0 22.2 %copy-start.3 = (f32[512,2048]{1,0:T(8,128)S(1)}, f32[512,2048]{1,0:T(8,128)}, u32[]{:S(2)}) copy-start(f32[512,2048]{1,0:T(8,128)} %param.8) | copy-start | bytes 12582916
  1030.9 210.4 %all-gather.11.cloned.1.call-start = ((), (), s32[]{:S(2)}) async-start(), calls=%async_computation.11 | async-start | bytes 18874368 | tf_op jit(solution)/shard_map/all_gather | solution.py:61
Sparse Core Ops, SparseCore 0:
  119.1 40.9 all-reduce.4
  162.0 36.6 all-gather.4
  235.5 38.2 all-reduce.6
  410.9 115.9 reduce-scatter.2
  530.4 89.8 all-gather.6
  741.9 38.2 all-reduce.8
  782.1 36.6 all-gather.8
  855.6 38.2 all-reduce.10
  1031.0 115.9 reduce-scatter.4
  1151.4 89.8 all-gather.10
where the time goes:
time: 1280 us; the launch traced here: 1270 us
  waiting for transfers between devices  636 us (50%)
  matrix products  536 us (42%)
  other arithmetic  52.1 us (4%)
  local copies, waits for them, and re-layouts  26.8 us (2%)
  between operations  14 us (1%)
    dot_general x2, matrix products, encode_partial(): jnp.dot(block.reshape(batch * vrows, cwidth), conduction_points, precisio...  234 us
    dot_general x2, matrix products, kernel_partial(): lax.dot_general(weighted.reshape(batch * vrows, prows), conduction_points...  229 us
    reduce_scatter x2, waiting for transfers between devices, chebyshev(): lax.psum_scatter(partial_value, 'pts', scatter_dimension=2, tiled=True)  223 us
    all_gather x2, waiting for transfers between devices, chebyshev(): return lax.all_gather(result, 'pts', axis=2, tiled=True)  180 us
    psum x2, waiting for transfers between devices, source_points(): summed = lax.psum(partial_value, 'orb')  79.5 us
    all_gather x2, waiting for transfers between devices, source_points(): encoded = lax.all_gather(summed, 'pts', axis=1, tiled=True)  77.1 us
    psum x2, waiting for transfers between devices, kernel_partial(): interacted = lax.psum(local_terms, 'orb')  76.8 us
    dot_general x2, matrix products, kernel_partial(): lax.dot_general(chosen, screened, (((1,), (1,)), ((), ())), precision=hig...  73.3 us
  transfers between devices with their start and end apart: 10, of which 10 were waited for; matrix products, arithmetic and copies ran while one was open for 1% of the time, Pallas kernels for 0%

commit v1 on v0

v1 whole, which is shorter than its diff:
```python
import functools

import jax
import jax.numpy as jnp
from jax import lax
from jax.experimental import pallas as pl
from jax.experimental.pallas import tpu as pltpu
from jax.sharding import PartitionSpec as P

center_shift = 2.5
f32, bf16 = jnp.float32, jnp.bfloat16
plain = (((1,), (0,)), ((), ()))
across = (((1,), (1,)), ((), ()))
anywhere = pl.BlockSpec(memory_space=pl.ANY)
vmem_bytes = 56 * 2**20
chunks = 4


def params():
    return pltpu.CompilerParams(vmem_limit_bytes=vmem_bytes)


def cost(flops, nbytes):
    return pl.CostEstimate(flops=flops // 16, bytes_accessed=nbytes // 16, transcendentals=0)


def split(x):
    hi = x.astype(bf16)
    return hi, (x - hi.astype(f32)).astype(bf16)


def dot(a, b, dims=plain):
    return lax.dot_general(a, b, dims, preferred_element_type=f32)


def part_of(batch, rows):
    return max(k for k in range(1, batch + 1) if batch % k == 0 and (k == 1 or k * rows <= 512))


def call(kernel, name, grid, in_specs, out_specs, out_shape, scratch, estimate, args, after):
    count = len(args)

    def run(*refs):
        kernel(*refs[:count], *refs[count + len(after) :])

    return pl.pallas_call(
        run,
        grid_spec=pltpu.PrefetchScalarGridSpec(
            num_scalar_prefetch=1,
            grid=grid,
            in_specs=in_specs + [anywhere] * len(after),
            out_specs=out_specs,
            scratch_shapes=scratch,
        ),
        out_shape=out_shape,
        compiler_params=params(),
        cost_estimate=estimate,
        name=name,
    )(*args, *after)


def encode_own_kernel(part, at_ref, x_ref, c_ref, v_ref, o_ref, xs, cs, whole):
    batch, vrows, cwidth = x_ref.shape
    width = o_ref.shape[3]

    @pl.when(pl.program_id(0) == 0)
    def _():
        hi, lo = split(c_ref[...])
        cs[0:cwidth] = hi
        cs[cwidth : 2 * cwidth] = lo
        cs[2 * cwidth :] = hi

    hi, lo = split(x_ref[...].reshape(batch * vrows, cwidth))
    xs[:, 0:cwidth] = hi
    xs[:, cwidth : 2 * cwidth] = hi
    xs[:, 2 * cwidth :] = lo
    v = v_ref[...]
    for i in range(batch // part):
        prod = dot(xs[i * part * vrows : (i + 1) * part * vrows, :], cs[...])
        prod = prod.reshape(part, vrows, v.shape[1]) * v[None]
        whole[i * part : (i + 1) * part, :] = jnp.sum(prod, axis=1)
    for j in range(2):
        o_ref[j, 0] = whole[:, pl.ds(pl.multiple_of((at_ref[1] ^ j) * width, width), width)]


def encode_own(x, c, v, at, start, count, size, after):
    vrows, cwidth = x.shape[1:]
    points = c.shape[1]
    width = points // 2
    return call(
        functools.partial(encode_own_kernel, part_of(size, vrows)),
        "encode_own",
        (count,),
        [
            pl.BlockSpec((size, vrows, cwidth), lambda i, at: ((start + i) ^ at[0], 0, 0)),
            pl.BlockSpec((cwidth, points), lambda i, at: (0, 0)),
            pl.BlockSpec((vrows, points), lambda i, at: (0, 0)),
        ],
        pl.BlockSpec((2, 1, size, width), lambda i, at: (0, i, 0, 0)),
        jax.ShapeDtypeStruct((2, count, size, width), f32),
        [
            pltpu.VMEM((size * vrows, 3 * cwidth), bf16),
            pltpu.VMEM((3 * cwidth, points), bf16),
            pltpu.VMEM((size, points), f32),
        ],
        cost(6 * size * count * vrows * cwidth * points, 4 * size * count * vrows * cwidth),
        (at, x, c, v),
        after,
    )


def encode_all_kernel(part, at_ref, x_ref, hi_ref, lo_ref, v_ref, o_ref, xs):
    del at_ref
    batch, vrows, cwidth = x_ref.shape

    @pl.when((pl.program_id(0) == 0) & (pl.program_id(1) == 0))
    def _():
        hi, lo = split(x_ref[...].reshape(batch * vrows, cwidth))
        xs[:, 0:cwidth] = hi
        xs[:, cwidth : 2 * cwidth] = hi
        xs[:, 2 * cwidth :] = lo

    chi = hi_ref[0]
    w = jnp.concatenate([chi, lo_ref[0], chi], axis=0)
    v = v_ref[0]
    for i in range(batch // part):
        prod = dot(xs[i * part * vrows : (i + 1) * part * vrows, :], w)
        prod = prod.reshape(part, vrows, v.shape[1]) * v[None]
        o_ref[0, 0, i * part : (i + 1) * part, :] = jnp.sum(prod, axis=1)


def slot_of(d, n):
    return group_of(d) + ((d // 2) % 2) * (n // 2)


def group_of(d):
    return (d // 4) * 2 + d % 2


def encode_all(x, chi, clo, v, at, which, n, no, after):
    batch, vrows, cwidth = x.shape
    width = chi.shape[2] // 2
    per = n // no

    def piece(e, c, at):
        return (slot_of(((at[3] ^ e) * per + c) ^ at[2], n), 0, which ^ at[1])

    return call(
        functools.partial(encode_all_kernel, part_of(batch, vrows)),
        "encode_all",
        (no, per),
        [
            pl.BlockSpec((batch, vrows, cwidth), lambda e, c, at: (0, 0, 0)),
            pl.BlockSpec((1, cwidth, width), piece),
            pl.BlockSpec((1, cwidth, width), piece),
            pl.BlockSpec((1, vrows, width), piece),
        ],
        pl.BlockSpec((1, 1, batch, width), lambda e, c, at: (e, c, 0, 0)),
        jax.ShapeDtypeStruct((no, per, batch, width), f32),
        [pltpu.VMEM((batch * vrows, 3 * cwidth), bf16)],
        cost(6 * batch * vrows * cwidth * width * n, 4 * (cwidth + vrows) * width * n),
        (at, x, chi, clo, v),
        after,
    )


def interact_kernel(order, at_ref, e_ref, s_ref, o_ref, whole, es):
    n, per, size, width = e_ref.shape
    batch = whole.shape[0]

    @pl.when(pl.program_id(0) == 0)
    def _():
        for i, d in enumerate(order):
            row = group_of(d) * size
            for c in range(per):
                column = (2 * c + (at_ref[1] ^ ((d // 2) % 2))) * width
                whole[row : row + size, pl.ds(pl.multiple_of(column, width), width)] = e_ref[i, c]
        hi, lo = split(whole[...])
        es[0:batch] = hi
        es[batch:] = lo

    hi, lo = split(s_ref[...])
    both = dot(es[...], hi, across)
    result = both[:batch] + both[batch:] + dot(es[0:batch], lo, across)
    for g in range(batch // size):
        o_ref[0, g] = result[g * size : (g + 1) * size]


def interact(e, s, at, after):
    n, per, size, width = e.shape
    rows, columns = s.shape
    batch = n // 2 * size
    no = n // per
    tile = rows // no
    return call(
        functools.partial(interact_kernel, slots(spread_bits(n))),
        "interact",
        (no,),
        [
            pl.BlockSpec(e.shape, lambda i, at: (0, 0, 0, 0)),
            pl.BlockSpec((tile, columns), lambda i, at: (i ^ at[3], 0)),
        ],
        pl.BlockSpec((1, n // 2, size, tile), lambda i, at: (i, 0, 0, 0)),
        jax.ShapeDtypeStruct((no, n // 2, size, tile), f32),
        [pltpu.VMEM((batch, columns), f32), pltpu.VMEM((2 * batch, columns), bf16)],
        cost(6 * batch * columns * rows, 4 * columns * rows),
        (at, e, s),
        after,
    )


def decode_kernel(part, start, factor, at_ref, y_ref, hi_ref, lo_ref, v_ref, ve_ref, ce_ref, *refs):
    block_ref, o_ref, whole = refs[0], refs[-2], refs[-1]
    batch, vrows, cwidth = o_ref.shape
    tiles, tile = y_ref.shape[0], y_ref.shape[3]

    @pl.when(pl.program_id(0) == 0)
    def _():
        o_ref[...] = jnp.zeros_like(o_ref)

    for e in range(tiles):
        if tiles == 1:
            whole[...] = y_ref[e, 0]
        else:
            whole[:, pl.ds(pl.multiple_of((e ^ at_ref[3]) * tile, tile), tile)] = y_ref[e, 0]
    v = v_ref[0]
    chi, clo = hi_ref[0], lo_ref[0]
    for i in range(batch // part):
        y = whole[start + i * part : start + (i + 1) * part, :]
        weighted = (y[:, None, :] * v[None]).reshape(part * vrows, v.shape[1])
        hi, lo = split(weighted)
        got = dot(hi, chi, across) + dot(hi, clo, across) + dot(lo, chi, across)
        o_ref[i * part : (i + 1) * part] += got.reshape(part, vrows, cwidth)

    @pl.when(pl.program_id(0) == pl.num_programs(0) - 1)
    def _():
        shifted = (ce_ref[...] - ve_ref[...]) - center_shift
        result = factor * (o_ref[...] + shifted[None] * block_ref[...])
        if len(refs) > 3:
            result = result - refs[1][...]
        o_ref[...] = result


def decode(y, chi, clo, v, ve, ce, at, amplitudes, first, chunk, chunks, factor, after):
    tiles, pieces, size, tile = y.shape
    points = tiles * tile
    batch = size // chunks
    vrows, cwidth = v.shape[1], chi.shape[1]
    own = pl.BlockSpec((batch, vrows, cwidth), lambda p, at: (at[0] * chunks + chunk, 0, at[1]))
    mine = pl.BlockSpec((batch, vrows, cwidth), lambda p, at: (chunk, 0, 0))
    blocks = [amplitudes] if first is None else [first, amplitudes]
    return call(
        functools.partial(decode_kernel, part_of(batch, vrows), chunk * batch, factor),
        "decode",
        (pieces,),
        [
            pl.BlockSpec((tiles, 1, size, tile), lambda p, at: (0, p, 0, 0)),
            pl.BlockSpec((1, cwidth, points), lambda p, at: (p, 0, 0)),
            pl.BlockSpec((1, cwidth, points), lambda p, at: (p, 0, 0)),
            pl.BlockSpec((1, vrows, points), lambda p, at: (p, 0, 0)),
            pl.BlockSpec((vrows, 1), lambda p, at: (0, 0)),
            pl.BlockSpec((1, cwidth), lambda p, at: (0, at[1])),
        ]
        + ([own] if first is None else [mine, own]),
        pl.BlockSpec((batch, vrows, cwidth), lambda p, at: (0, 0, 0)),
        jax.ShapeDtypeStruct((batch, vrows, cwidth), f32),
        [pltpu.VMEM((size, points), f32)],
        cost(6 * batch * vrows * cwidth * points * pieces, 4 * (cwidth + vrows) * points * pieces),
        (at, y, chi, clo, v, ve, ce, *blocks),
        after,
    )


def place_kernel(c_ref, v_ref, *refs):
    hi_ref, lo_ref, o_ref = refs[-3:]
    hi, lo = split(c_ref[...])
    hi_ref[0] = hi
    lo_ref[0] = lo
    o_ref[0] = v_ref[...]


def place(piece, vpiece, slot, so_far, n):
    cwidth, points = piece.shape
    vrows = vpiece.shape[0]
    tile = min(points, 512)
    carried = [] if so_far is None else list(so_far)
    rows = [cwidth, cwidth, vrows]
    return pl.pallas_call(
        place_kernel,
        grid=(points // tile,),
        in_specs=[pl.BlockSpec((r, tile), lambda j: (0, j)) for r in rows[1:]]
        + [anywhere] * len(carried),
        out_specs=[pl.BlockSpec((1, r, tile), lambda j: (slot, 0, j)) for r in rows],
        out_shape=[
            jax.ShapeDtypeStruct((n, r, points), t) for r, t in zip(rows, (bf16, bf16, f32))
        ],
        input_output_aliases={2 + i: i for i in range(len(carried))},
        compiler_params=params(),
        cost_estimate=cost(0, 8 * (cwidth + vrows) * points),
        name="place",
    )(piece, vpiece, *carried)


def put_kernel(owners, chunk, chunks, count, at_ref, *refs):
    pieces, out, held, came, went = refs[:count], refs[-4], refs[-3], refs[-2], refs[-1]
    batch, _, cwidth = pieces[0].shape
    arriving = [pltpu.make_async_copy(pieces[i], held.at[i], came.at[i]) for i in range(count)]
    for copy in arriving:
        copy.start()
    leaving = []
    for i, d in enumerate(owners):
        team, half = at_ref[0] ^ group_of(d), at_ref[1] ^ ((d // 2) % 2)
        where = out.at[
            pl.ds((team * chunks + chunk) * batch, batch),
            :,
            pl.ds(pl.multiple_of(half * cwidth, cwidth), cwidth),
        ]
        arriving[i].wait()
        leaving.append(pltpu.make_async_copy(held.at[i], where, went.at[i]))
        leaving[i].start()
    for copy in leaving:
        copy.wait()


def put(pieces, chunk, chunks, at, so_far, shape):
    owners = sorted(pieces)
    count = len(owners)
    carried = [] if so_far is None else [so_far]
    block = pieces[owners[0]].shape
    return pl.pallas_call(
        functools.partial(put_kernel, owners, chunk, chunks, count),
        in_specs=[pl.BlockSpec(memory_space=pltpu.SMEM)] + [anywhere] * (count + len(carried)),
        out_specs=anywhere,
        out_shape=jax.ShapeDtypeStruct(shape, f32),
        scratch_shapes=[
            pltpu.VMEM((count,) + block, f32),
            pltpu.SemaphoreType.DMA((count,)),
            pltpu.SemaphoreType.DMA((count,)),
        ],
        input_output_aliases={count + 1 + i: i for i in range(len(carried))},
        compiler_params=params(),
        cost_estimate=cost(0, 8 * count * pieces[owners[0]].size),
        name="put",
    )(at, *[pieces[d] for d in owners], *carried)


def flip(x, axis, bit, size):
    return lax.ppermute(x, axis, [(i, i ^ bit) for i in range(size)])


def bits_of(size):
    return [1 << i for i in range(size.bit_length() - 1)]


def reorder(x, dim, by):
    for bit in bits_of(x.shape[dim]):
        shape = x.shape[:dim] + (x.shape[dim] // (2 * bit), 2, bit) + x.shape[dim + 1 :]
        swapped = lax.rev(x.reshape(shape), (dim + 1,)).reshape(x.shape)
        x = jnp.where((by // bit) % 2 == 1, swapped, x)
    return x


def tie(x, after):
    return lax.optimization_barrier((x, after))[0]


def take_bit(x, dim, bit, value):
    shape = x.shape[:dim] + (x.shape[dim] // (2 * bit), 2, bit) + x.shape[dim + 1 :]
    part = lax.index_in_dim(x.reshape(shape), value, dim + 1, keepdims=False)
    return part.reshape(x.shape[:dim] + (x.shape[dim] // 2,) + x.shape[dim + 1 :])


def scatter_sum(x, axis, size):
    for bit in reversed(bits_of(size)):
        sent = flip(x[bit:], axis, bit, size)
        x = x[:bit] + sent
    return x[0]


def collect(x, axis, size, order):
    x = x[None]
    got = {0: x[0]}
    done = []
    for bit in order:
        for d in list(got):
            got[d | bit] = flip(got[d], axis, bit, size)
        done.append(bit)
    return [got[d] for d in range(size)]


class Comm:
    def __init__(self, n, no):
        self.n, self.no = n, no
        self.me, self.mo = lax.axis_index("pts"), lax.axis_index("orb")
        self.half = (self.me // 2) % 2
        self.member = group_of(self.me)
        self.per = n // no


def slots(order):
    found = [0]
    for bit in order:
        found = found + [d | bit for d in found]
    return found


def spread_bits(n):
    return [2] + [b for b in bits_of(n) if b >= 4] + [1]


def spread_encoded(x, comm):
    x = x[None]
    for bit in spread_bits(comm.n):
        x = jnp.concatenate([x, flip(x, "pts", bit, comm.n)], axis=0)
    return x


def send_encoded_own(x, comm):
    n, no, per = comm.n, comm.no, comm.per
    x = x[None]
    for bit in bits_of(n):
        dim = 1 if bit == 2 else 2
        other = flip(take_bit(x, dim, 1, 1), "pts", bit, n)
        x = jnp.concatenate([take_bit(x, dim, 1, 0), other], axis=0)
    x = x[:, 0, 0].reshape((no, per) + x.shape[3:])
    x = reorder(x, 0, (comm.me // per) ^ comm.mo)
    if per > 1:
        x = reorder(x, 1, comm.me % per)
    return spread_encoded(scatter_sum(x, "orb", no), comm)


def send_encoded_all(send, keep, comm):
    x = keep + flip(send, "pts", 2, comm.n)
    return spread_encoded(scatter_sum(x, "orb", comm.no), comm)


def send_interacted(x, comm):
    n, no = comm.n, comm.no
    x = x[:, None]
    for bit in [b for b in bits_of(n) if b != 2]:
        other = flip(take_bit(x, 2, 1, 1), "pts", bit, n)
        x = jnp.concatenate([take_bit(x, 2, 1, 0), other], axis=1)
    x = scatter_sum(x[:, :, 0], "orb", no)[None]
    for bit in bits_of(no):
        x = jnp.concatenate([x, flip(x, "orb", bit, no)], axis=0)
    x = jnp.concatenate([x, flip(x, "pts", 2, n)], axis=1)
    if x.shape[3] % 128 == 0:
        return x
    x = reorder(x, 0, comm.mo).transpose(1, 2, 0, 3)
    return x.reshape((1,) + x.shape[:2] + (-1,))


def around(x, order, n):
    got = {0: x}
    stages = []
    for bit in order:
        new = {d | bit: flip(got[d], "pts", bit, n) for d in list(got)}
        got.update(new)
        stages.append(new)
    return got, stages


def body(
    amplitudes, valence_points, conduction_points, screened, valence_energy, conduction_energy, n, no
):
    comm = Comm(n, no)
    ve, ce = valence_energy[:, None], conduction_energy[None, :]
    teams = n // 2
    size = amplitudes.shape[0] // teams
    at = jnp.stack([comm.member, comm.half, comm.me, comm.mo]).astype(jnp.int32)

    cwidth = conduction_points.shape[0] // 2
    mine = lax.dynamic_slice_in_dim(conduction_points, comm.half * cwidth, cwidth, 0)
    other = lax.dynamic_slice_in_dim(conduction_points, (1 - comm.half) * cwidth, cwidth, 0)
    high = [b for b in bits_of(n) if b >= 4]

    pieces = {0: mine, 2: flip(other, "pts", 2, n)}
    vpieces = {0: valence_points, high[0]: flip(valence_points, "pts", high[0], n)}
    pieces[high[0]] = flip(mine, "pts", high[0], n)
    early = (pieces[2], pieces[high[0]])
    parts, after = [], ()
    runs = 4 if teams % 4 == 0 else 1
    for i in range(runs):
        part = encode_own(
            amplitudes,
            conduction_points,
            valence_points,
            at,
            i * (teams // runs),
            teams // runs,
            size,
            after + (early if i == runs - 1 else ()),
        )
        after = (part,)
        parts.append(part)
    part = jnp.concatenate(parts, axis=1)
    for bit in high:
        for d in list(pieces):
            if d | bit not in pieces:
                pieces[d | bit] = flip(pieces[d], "pts", bit, n)
    for bit in high[1:] + [2]:
        for d in list(vpieces):
            vpieces[d | bit] = flip(vpieces[d], "pts", bit, n)
    second = tuple(pieces[d] for d in pieces if d not in (0, 2, high[0]))
    second += tuple(vpieces[d] for d in vpieces if d != 0)
    e = send_encoded_own(part, comm)
    got = interact(e, screened, at, after + second)

    for d in list(pieces):
        pieces[d | 1] = flip(pieces[d], "pts", 1, n)
        vpieces[d | 1] = flip(vpieces[d], "pts", 1, n)
    placed = None
    for d in pieces:
        placed = place(pieces[d], vpieces[d], slot_of(d, n), placed, n)
    chi, clo, v = placed

    def decoded(y, first, chunk, chunks, factor, after):
        return decode(y, chi, clo, v, ve, ce, at, amplitudes, first, chunk, chunks, factor, after)

    y = send_interacted(got, comm)
    first = decoded(y, None, 0, 1, 0.5, ())
    send = encode_all(first, chi, clo, v, at, 1, n, no, ())
    keep = encode_all(first, chi, clo, v, at, 0, n, no, (send,))
    e = send_encoded_all(send, keep, comm)
    y = send_interacted(interact(e, screened, at, ()), comm)
    out, after = None, ()
    waiting = []
    for chunk in range(chunks):
        if chunk >= 2:
            after += tuple(waiting[chunk - 2][1][0].values())
        if chunk >= 3:
            after += tuple(waiting[chunk - 3][1][-1].values())
        got = decoded(y, first, chunk, chunks, 1.0, after)
        after = (got,)
        waiting.append(around(got, [2] + high if chunk % 2 == 0 else high + [2], n))
    for chunk, (near, _) in enumerate(waiting):
        out = put(near, chunk, chunks, at, out, amplitudes.shape)
        far = {d | 1: flip(near[d], "pts", 1, n) for d in near}
        out = put(far, chunk, chunks, at, out, amplitudes.shape)
    return out


def solution(mesh):
    n, no = mesh.shape["pts"], mesh.shape["orb"]
    return jax.shard_map(
        functools.partial(body, n=n, no=no),
        mesh=mesh,
        in_specs=(
            P(None, "orb", None),
            P("orb", "pts"),
            P(None, "pts"),
            P("pts", "orb"),
            P("orb"),
            P(),
        ),
        out_specs=P(None, "orb", None),
        check_vma=False,
    )
```

time: 1280 us -> 697 us (0.54)
  matrix products: 536 us -> 0 us
  waiting for transfers between devices: 636 us -> 258 us
  Pallas kernels: 0 us -> 366 us
  other arithmetic: 52.1 us -> 8.91 us
  starting transfers between devices: 0.37 us -> 39.6 us
  local copies, waits for them, and re-layouts: 26.8 us -> 13.2 us
  between operations: 14 us -> 1.15 us
    dot_general x6 -> x0, matrix products: 536 us -> none  [the longest x2 234 us: encode_partial(): jnp.dot(block.reshape(batch * vrows, cwidth), conduction_points, precisio...]
    pallas_call x0 -> x29, Pallas kernels: none -> 366 us  [the longest x13 308 us: call(): pl.pallas_call(run, grid_spec=pltpu.PrefetchScalarGridSpec(num_scalar_pre...]
    ppermute x0 -> x70, waiting for transfers between devices: none -> 258 us  [flip(): return lax.ppermute(x, axis, [(i, i ^ bit) for i in range(size)])]
    all_gather x4 -> x0, waiting for transfers between devices: 257 us -> none  [the longest x2 180 us: chebyshev(): return lax.all_gather(result, 'pts', axis=2, tiled=True)]
    reduce_scatter x2 -> x0, waiting for transfers between devices: 223 us -> none  [chebyshev(): lax.psum_scatter(partial_value, 'pts', scatter_dimension=2, tiled=True)]
    psum x4 -> x0, waiting for transfers between devices: 156 us -> none  [the longest x2 79.5 us: source_points(): summed = lax.psum(partial_value, 'orb')]
    dot_general x2 -> x0, other arithmetic: 44.5 us -> none  [kernel_partial(): lax.dot_general(weighted.reshape(batch * vrows, prows), conduction_points...]
    ppermute x0 -> x70, starting transfers between devices: none -> 39.6 us  [flip(): return lax.ppermute(x, axis, [(i, i ^ bit) for i in range(size)])]
  transfers between devices with their start and end apart: 10 -> 70, of which waited for: 10 -> 32; matrix products, arithmetic and copies ran while one was open for 1% -> 1% of each run, Pallas kernels for 0% -> 28%
where the time goes in v1:
time: 697 us; the launch traced here: 687 us
  Pallas kernels  366 us (53%)
  waiting for transfers between devices  258 us (37%)
  starting transfers between devices  39.6 us (6%)
  local copies, waits for them, and re-layouts  13.2 us (2%)
  other arithmetic  8.91 us (1%)
    pallas_call x13, Pallas kernels, call(): pl.pallas_call(run, grid_spec=pltpu.PrefetchScalarGridSpec(num_scalar_pre...  308 us
    ppermute x70, waiting for transfers between devices, flip(): return lax.ppermute(x, axis, [(i, i ^ bit) for i in range(size)])  258 us
    ppermute x70, starting transfers between devices, flip(): return lax.ppermute(x, axis, [(i, i ^ bit) for i in range(size)])  39.6 us
    pallas_call x8, Pallas kernels, place(): pl.pallas_call(place_kernel, grid=(points // tile,), in_specs=[pl.BlockSp...  33.4 us
    pallas_call x8, Pallas kernels, put(): pl.pallas_call(functools.partial(put_kernel, owners, chunk, chunks, count...  24.7 us
  transfers between devices with their start and end apart: 70, of which 32 were waited for; matrix products, arithmetic and copies ran while one was open for 1% of the time, Pallas kernels for 28%

profile of v1, /device:TPU:0, one launch (start us, length us, event | category | flops | bytes accessed | tf_op | source)
XLA Modules:
  0.0 686.9 jit_solution(13975507957044934282)
XLA Ops:
  9.8 18.2 %encode_own.4.refs_4_ = f32[2,1,16,1024]{3,2,1,0:T(8,128)} custom-call(s32[4]{0:T(128)} %pad_add_fusion.refs_0_.at_ref, f32[64,128,512]{2,1,0:T(8,128)} %refs_8_.7, f32[512,2048]{1,0:T(8,128)} %refs_2_.9, f32[128,2048]{1,0:T(8,128)} %v_ref.1), custom_call_target="tpu_custom_call" | custom-call | flops 805306368 | bytes 262144 | tf_op jit(solution)/shard_map/encode_own/pallas_call | solution.py:46
  28.0 18.6 %encode_own.5.refs_4_ = f32[2,1,16,1024]{3,2,1,0:T(8,128)} custom-call(s32[4]{0:T(128)} %pad_add_fusion.refs_0_.at_ref, f32[64,128,512]{2,1,0:T(8,128)} %refs_8_.7, f32[512,2048]{1,0:T(8,128)} %refs_2_.9, f32[128,2048]{1,0:T(8,128)} %v_ref.1, f32[2,1,16,1024]{3,2,1,0:T(8,128)} %encode_own.4.refs_4_), custom_call_target="tpu_custom_call" | custom-call | flops 805306368 | bytes 262144 | tf_op jit(solution)/shard_map/encode_own/pallas_call | solution.py:46
  46.5 18.3 %encode_own.6.refs_4_ = f32[2,1,16,1024]{3,2,1,0:T(8,128)} custom-call(s32[4]{0:T(128)} %pad_add_fusion.refs_0_.at_ref, f32[64,128,512]{2,1,0:T(8,128)} %refs_8_.7, f32[512,2048]{1,0:T(8,128)} %refs_2_.9, f32[128,2048]{1,0:T(8,128)} %v_ref.1, f32[2,1,16,1024]{3,2,1,0:T(8,128)} %encode_own.5.refs_4_), custom_call_target="tpu_custom_call" | custom-call | flops 805306368 | bytes 262144 | tf_op jit(solution)/shard_map/encode_own/pallas_call | solution.py:46
  66.2 18.2 %encode_own.7.refs_3_ = f32[2,1,16,1024]{3,2,1,0:T(8,128)} custom-call(s32[4]{0:T(128)} %pad_add_fusion.refs_0_.at_ref, f32[64,128,512]{2,1,0:T(8,128)} %refs_8_.7, f32[512,2048]{1,0:T(8,128)} %refs_2_.9, f32[128,2048]{1,0:T(8,128)} %v_ref.1, f32[2,1,16,1024]{3,2,1,0:T(8,128)} %encode_own.6.refs_4_, f32[256,2048]{1,0:T(8,128)} %collective-permute-done.refs_5_.c_ref, ...), custom_call_target="tpu_custom_call" | custom-call | flops 805306368 | bytes 262144 | tf_op jit(solution)/shard_map/encode_own/pallas_call | solution.py:46
  108.8 8.5 %collective-permute-done.5 = f32[2,2,16,1024]{3,2,1,0:T(8,128)S(1)} collective-permute-done((f32[2,2,16,1024]{3,2,1,0:T(8,128)S(1)}, f32[2,2,16,1024]{3,2,1,0:T(8,128)S(1)}, u32[]{:S(2)}, u32[]{:S(2)}) %collective-permute-start.5) | collective-permute-done | bytes 262176 | tf_op jit(solution)/shard_map/ppermute | solution.py:348
  133.4 47.1 %collective-permute-done.8 = f32[2,2,16,1024]{3,2,1,0:T(8,128)S(1)} collective-permute-done((f32[2,2,16,1024]{3,2,1,0:T(8,128)S(1)}, f32[2,2,16,1024]{3,2,1,0:T(8,128)S(1)}, u32[]{:S(2)}, u32[]{:S(2)}) %collective-permute-start.8) | collective-permute-done | bytes 262176 | tf_op jit(solution)/shard_map/ppermute | solution.py:348
  186.8 17.2 %interact.2 = f32[4,4,16,512]{3,2,1,0:T(8,128)} custom-call(s32[4]{0:T(128)} %pad_add_fusion.refs_0_.at_ref, f32[8,2,16,1024]{3,2,1,0:T(8,128)} %pad_maximum_fusion.refs_1_, f32[2048,4096]{1,0:T(8,128)} %refs_2_.11, f32[2,1,16,1024]{3,2,1,0:T(8,128)} %encode_own.7.refs_3_, f32[256,2048]{1,0:T(8,128)} %copy-done.3, f32[128,2048]{1,0:T(8,128)} %copy-done.5, ...), custom_call_target="tpu_custom_call" | custom-call | flops 201326592 | bytes 2097152 | tf_op jit(solution)/shard_map/interact/pallas_call | solution.py:46
  215.7 13.7 %collective-permute-done.16 = f32[2,4,16,512]{3,2,1,0:T(8,128)S(1)} collective-permute-done((f32[2,4,16,512]{3,2,1,0:T(8,128)S(1)}, f32[2,4,16,512]{3,2,1,0:T(8,128)S(1)}, u32[]{:S(2)}, u32[]{:S(2)}) %collective-permute-start.16) | collective-permute-done | bytes 262176 | tf_op jit(solution)/shard_map/ppermute | solution.py:348
  241.3 14.2 %collective-permute-done.19 = f32[2,4,16,512]{3,2,1,0:T(8,128)S(1)} collective-permute-done((f32[2,4,16,512]{3,2,1,0:T(8,128)S(1)}, f32[2,4,16,512]{3,2,1,0:T(8,128)S(1)}, u32[]{:S(2)}, u32[]{:S(2)}) %collective-permute-start.19) | collective-permute-done | bytes 262176 | tf_op jit(solution)/shard_map/ppermute | solution.py:348
  292.6 59.5 %decode.5.refs_1_.refs_7_ = f32[16,128,256]{2,1,0:T(8,128)} custom-call(s32[4]{0:T(128)} %pad_add_fusion.refs_0_.at_ref, f32[4,8,16,512]{3,2,1,0:T(8,128)} %pad_maximum_fusion.1.refs_1_, bf16[8,256,2048]{2,1,0:T(8,128)(2,1)} %get-tuple-element.50.refs_2_, bf16[8,256,2048]{2,1,0:T(8,128)(2,1)} %get-tuple-element.51.refs_3_, ...), custom_call_target="tpu_custom_call" | custom-call | flops 3221225472 | bytes 1572864 | tf_op jit(solution)/shard_map/decode/pallas_call | solution.py:46
  352.1 32.2 %encode_all.2.refs_5_ = f32[4,2,16,1024]{3,2,1,0:T(8,128)} custom-call(s32[4]{0:T(128)} %pad_add_fusion.refs_0_.at_ref, f32[16,128,256]{2,1,0:T(8,128)} %decode.5.refs_1_.refs_7_, bf16[8,256,2048]{2,1,0:T(8,128)(2,1)} %get-tuple-element.50.refs_2_, bf16[8,256,2048]{2,1,0:T(8,128)(2,1)} %get-tuple-element.51.refs_3_, f32[8,128,2048]{2,1,0:T(8,128)} %get-tuple-element.52.refs_4_), custom_call_target="tpu_custom_call" | custom-call | flops 1610612736 | bytes 786432 | tf_op jit(solution)/shard_map/encode_all/pallas_call | solution.py:46
  385.8 32.1 %encode_all.3 = f32[4,2,16,1024]{3,2,1,0:T(8,128)} custom-call(s32[4]{0:T(128)} %pad_add_fusion.refs_0_.at_ref, f32[16,128,256]{2,1,0:T(8,128)} %decode.5.refs_1_.refs_7_, bf16[8,256,2048]{2,1,0:T(8,128)(2,1)} %get-tuple-element.50.refs_2_, bf16[8,256,2048]{2,1,0:T(8,128)(2,1)} %get-tuple-element.51.refs_3_, f32[8,128,2048]{2,1,0:T(8,128)} %get-tuple-element.52.refs_4_, ...), custom_call_target="tpu_custom_call" | custom-call | flops 1610612736 | bytes 786432 | tf_op jit(solution)/shard_map/encode_all/pallas_call | solution.py:46
  419.1 13.7 %collective-permute-done.30 = f32[2,2,16,1024]{3,2,1,0:T(8,128)S(1)} collective-permute-done((f32[2,2,16,1024]{3,2,1,0:T(8,128)S(1)}, f32[2,2,16,1024]{3,2,1,0:T(8,128)S(1)}, u32[]{:S(2)}, u32[]{:S(2)}) %collective-permute-start.30) | collective-permute-done | bytes 262176 | tf_op jit(solution)/shard_map/ppermute | solution.py:348
  452.9 17.2 %interact.3 = f32[4,4,16,512]{3,2,1,0:T(8,128)} custom-call(s32[4]{0:T(128)} %pad_add_fusion.refs_0_.at_ref, f32[8,2,16,1024]{3,2,1,0:T(8,128)} %pad_maximum_fusion.2.refs_1_, f32[2048,4096]{1,0:T(8,128)} %refs_2_.11), custom_call_target="tpu_custom_call" | custom-call | flops 201326592 | bytes 2097152 | tf_op jit(solution)/shard_map/interact/pallas_call | solution.py:46
  482.5 12.8 %collective-permute-done.37 = f32[2,4,16,512]{3,2,1,0:T(8,128)S(1)} collective-permute-done((f32[2,4,16,512]{3,2,1,0:T(8,128)S(1)}, f32[2,4,16,512]{3,2,1,0:T(8,128)S(1)}, u32[]{:S(2)}, u32[]{:S(2)}) %collective-permute-start.37) | collective-permute-done | bytes 262176 | tf_op jit(solution)/shard_map/ppermute | solution.py:348
  506.9 11.8 %collective-permute-done.40 = f32[2,4,16,512]{3,2,1,0:T(8,128)S(1)} collective-permute-done((f32[2,4,16,512]{3,2,1,0:T(8,128)S(1)}, f32[2,4,16,512]{3,2,1,0:T(8,128)S(1)}, u32[]{:S(2)}, u32[]{:S(2)}) %collective-permute-start.40) | collective-permute-done | bytes 262176 | tf_op jit(solution)/shard_map/ppermute | solution.py:348
  519.4 13.3 %collective-permute-done.41 = f32[4,4,16,512]{3,2,1,0:T(8,128)S(1)} collective-permute-done((f32[4,4,16,512]{3,2,1,0:T(8,128)S(1)}, f32[4,4,16,512]{3,2,1,0:T(8,128)S(1)}, u32[]{:S(2)}, u32[]{:S(2)}) %collective-permute-start.41) | collective-permute-done | bytes 524320 | tf_op jit(solution)/shard_map/ppermute | solution.py:348
  533.7 19.2 %decode.6.refs_9_.refs_0_ = f32[4,128,256]{2,1,0:T(8,128)} custom-call(s32[4]{0:T(128)} %pad_add_fusion.refs_0_.at_ref, f32[4,8,16,512]{3,2,1,0:T(8,128)} %pad_maximum_fusion.3.refs_1_, bf16[8,256,2048]{2,1,0:T(8,128)(2,1)} %get-tuple-element.50.refs_2_, bf16[8,256,2048]{2,1,0:T(8,128)(2,1)} %get-tuple-element.51.refs_3_, ...), custom_call_target="tpu_custom_call" | custom-call | flops 805306368 | bytes 1572864 | tf_op jit(solution)/shard_map/decode/pallas_call | solution.py:46
  554.0 19.0 %decode.7.refs_9_.refs_0_ = f32[4,128,256]{2,1,0:T(8,128)} custom-call(s32[4]{0:T(128)} %pad_add_fusion.refs_0_.at_ref, f32[4,8,16,512]{3,2,1,0:T(8,128)} %pad_maximum_fusion.3.refs_1_, bf16[8,256,2048]{2,1,0:T(8,128)(2,1)} %get-tuple-element.50.refs_2_, bf16[8,256,2048]{2,1,0:T(8,128)(2,1)} %get-tuple-element.51.refs_3_, ...), custom_call_target="tpu_custom_call" | custom-call | flops 805306368 | bytes 1572864 | tf_op jit(solution)/shard_map/decode/pallas_call | solution.py:46
  576.9 19.0 %decode.8.refs_9_.refs_0_ = f32[4,128,256]{2,1,0:T(8,128)} custom-call(s32[4]{0:T(128)} %pad_add_fusion.refs_0_.at_ref, f32[4,8,16,512]{3,2,1,0:T(8,128)} %pad_maximum_fusion.3.refs_1_, bf16[8,256,2048]{2,1,0:T(8,128)(2,1)} %get-tuple-element.50.refs_2_, bf16[8,256,2048]{2,1,0:T(8,128)(2,1)} %get-tuple-element.51.refs_3_, ...), custom_call_target="tpu_custom_call" | custom-call | flops 805306368 | bytes 1572864 | tf_op jit(solution)/shard_map/decode/pallas_call | solution.py:46
  600.5 19.0 %decode.9.refs_0_ = f32[4,128,256]{2,1,0:T(8,128)} custom-call(s32[4]{0:T(128)} %pad_add_fusion.refs_0_.at_ref, f32[4,8,16,512]{3,2,1,0:T(8,128)} %pad_maximum_fusion.3.refs_1_, bf16[8,256,2048]{2,1,0:T(8,128)(2,1)} %get-tuple-element.50.refs_2_, bf16[8,256,2048]{2,1,0:T(8,128)(2,1)} %get-tuple-element.51.refs_3_, ...), custom_call_target="tpu_custom_call" | custom-call | flops 805306368 | bytes 1572864 | tf_op jit(solution)/shard_map/decode/pallas_call | solution.py:46
  623.1 11.2 %collective-permute-done.56.refs_2_ = f32[4,128,256]{2,1,0:T(8,128)S(1)} collective-permute-done((f32[4,128,256]{2,1,0:T(8,128)S(1)}, f32[4,128,256]{2,1,0:T(8,128)S(1)}, u32[]{:S(2)}, u32[]{:S(2)}) %collective-permute-start.56) | collective-permute-done | bytes 524320 | tf_op jit(solution)/shard_map/ppermute | solution.py:348
  637.2 8.4 %collective-permute-done.49.refs_2_ = f32[4,128,256]{2,1,0:T(8,128)S(1)} collective-permute-done((f32[4,128,256]{2,1,0:T(8,128)}, f32[4,128,256]{2,1,0:T(8,128)S(1)}, u32[]{:S(2)}, u32[]{:S(2)}) %collective-permute-start.49) | collective-permute-done | bytes 524320 | tf_op jit(solution)/shard_map/ppermute | solution.py:348
  646.3 9.7 %collective-permute-done.58.refs_3_ = f32[4,128,256]{2,1,0:T(8,128)S(1)} collective-permute-done((f32[4,128,256]{2,1,0:T(8,128)S(1)}, f32[4,128,256]{2,1,0:T(8,128)S(1)}, u32[]{:S(2)}, u32[]{:S(2)}) %collective-permute-start.58) | collective-permute-done | bytes 524320 | tf_op jit(solution)/shard_map/ppermute | solution.py:348
  (269 shorter events, 213.8 us)
Async XLA Ops:
  4.7 60.2 %collective-permute-start = (f32[256,2048]{1,0:T(8,128)}, f32[256,2048]{1,0:T(8,128)}, u32[]{:S(2)}, u32[]{:S(2)}) collective-permute-start(f32[256,2048]{1,0:T(8,128)} %get-tuple-element.54), channel_id=1, source_target_pairs={{0,8},{4,12},{8,0},{12,4},{16,24},{20,28},{24,16},{28,20},{1,9},{5... | collective-permute-start | bytes 6291464 | tf_op jit(solution)/shard_map/ppermute | solution.py:348
  7.7 57.2 %collective-permute-start.1 = (f32[256,2048]{1,0:T(8,128)}, f32[256,2048]{1,0:T(8,128)S(1)}, u32[]{:S(2)}, u32[]{:S(2)}) collective-permute-start(f32[256,2048]{1,0:T(8,128)} %get-tuple-element.53.c_ref), channel_id=1, source_target_pairs={{0,16},{4,20},{8,24},{12,28},{16,0},{20,4},{24,8},{28,12},{1,17},{... | collective-permute-start | bytes 6291464 | tf_op jit(solution)/shard_map/ppermute | solution.py:348
  106.7 26.1 %collective-permute-start.11 = (f32[128,2048]{1,0:T(8,128)S(1)}, f32[128,2048]{1,0:T(8,128)S(1)}, u32[]{:S(2)}, u32[]{:S(2)}) collective-permute-start(f32[128,2048]{1,0:T(8,128)S(1)} %copy-done), channel_id=1, source_target_pairs={{0,16},{4,20},{8,24},{12,28},{16,0},{20,4},{24,8},{28,12},{1,17},{... | collective-permute-start | bytes 3145736 | tf_op jit(solution)/shard_map/ppermute | solution.py:348
  107.2 77.3 %collective-permute-start.10 = (f32[256,2048]{1,0:T(8,128)}, f32[256,2048]{1,0:T(8,128)S(1)}, u32[]{:S(2)}, u32[]{:S(2)}) collective-permute-start(f32[256,2048]{1,0:T(8,128)} %collective-permute-done.refs_5_.c_ref), channel_id=1, source_target_pairs={{0,16},{4,20},{8,24},{12,28},{16,0},{20,4},{24,8},{28,12},{1,17},{... | collective-permute-start | bytes 6291464 | tf_op jit(solution)/shard_map/ppermute | solution.py:348
  127.4 53.0 %collective-permute-start.8 = (f32[2,2,16,1024]{3,2,1,0:T(8,128)S(1)}, f32[2,2,16,1024]{3,2,1,0:T(8,128)S(1)}, u32[]{:S(2)}, u32[]{:S(2)}) collective-permute-start(f32[2,2,16,1024]{3,2,1,0:T(8,128)S(1)} %pad_maximum_fusion.12), channel_id=1, source_target_pairs={{0,16},{4,20},{8,24},{12,28},{16,0},{20,4},{24,8},{28,12},{1,17},{... | collective-permute-start | bytes 786440 | tf_op jit(solution)/shard_map/ppermute | solution.py:348
  128.0 55.6 %collective-permute-start.12 = (f32[128,2048]{1,0:T(8,128)S(1)}, f32[128,2048]{1,0:T(8,128)S(1)}, u32[]{:S(2)}, u32[]{:S(2)}) collective-permute-start(f32[128,2048]{1,0:T(8,128)S(1)} %copy-done), channel_id=1, source_target_pairs={{0,8},{4,12},{8,0},{12,4},{16,24},{20,28},{24,16},{28,20},{1,9},{5... | collective-permute-start | bytes 3145736 | tf_op jit(solution)/shard_map/ppermute | solution.py:348
  132.8 50.7 %collective-permute-start.13 = (f32[128,2048]{1,0:T(8,128)S(1)}, f32[128,2048]{1,0:T(8,128)S(1)}, u32[]{:S(2)}, u32[]{:S(2)}) collective-permute-start(f32[128,2048]{1,0:T(8,128)S(1)} %collective-permute-done.11.refs_5_.v_ref), channel_id=1, source_target_pairs={{0,8},{4,12},{8,0},{12,4},{16,24},{20,28},{24,16},{28,20},{1,9},{5... | collective-permute-start | bytes 3145736 | tf_op jit(solution)/shard_map/ppermute | solution.py:348
  207.4 33.1 %collective-permute-start.27 = (f32[256,2048]{1,0:T(8,128)}, f32[256,2048]{1,0:T(8,128)}, u32[]{:S(2)}, u32[]{:S(2)}) collective-permute-start(f32[256,2048]{1,0:T(8,128)} %get-tuple-element.53.c_ref), channel_id=1, source_target_pairs={{0,4},{4,0},{8,12},{12,8},{16,20},{20,16},{24,28},{28,24},{1,5},{5... | collective-permute-start | bytes 6291464 | tf_op jit(solution)/shard_map/ppermute | solution.py:348
  207.4 27.1 %collective-permute-start.28 = (f32[128,2048]{1,0:T(8,128)S(1)}, f32[128,2048]{1,0:T(8,128)S(1)}, u32[]{:S(2)}, u32[]{:S(2)}) collective-permute-start(f32[128,2048]{1,0:T(8,128)S(1)} %copy-done), channel_id=1, source_target_pairs={{0,4},{4,0},{8,12},{12,8},{16,20},{20,16},{24,28},{28,24},{1,5},{5... | collective-permute-start | bytes 3145736 | tf_op jit(solution)/shard_map/ppermute | solution.py:348
  215.7 40.0 %collective-permute-start.25 = (f32[256,2048]{1,0:T(8,128)}, f32[256,2048]{1,0:T(8,128)}, u32[]{:S(2)}, u32[]{:S(2)}) collective-permute-start(f32[256,2048]{1,0:T(8,128)} %collective-permute-done.refs_5_.c_ref), channel_id=1, source_target_pairs={{0,4},{4,0},{8,12},{12,8},{16,20},{20,16},{24,28},{28,24},{1,5},{5... | collective-permute-start | bytes 6291464 | tf_op jit(solution)/shard_map/ppermute | solution.py:348
  234.5 47.6 %collective-permute-start.23 = (f32[256,2048]{1,0:T(8,128)S(1)}, f32[256,2048]{1,0:T(8,128)}, u32[]{:S(2)}, u32[]{:S(2)}) collective-permute-start(f32[256,2048]{1,0:T(8,128)S(1)} %copy-done.2), channel_id=1, source_target_pairs={{0,4},{4,0},{8,12},{12,8},{16,20},{20,16},{24,28},{28,24},{1,5},{5... | collective-permute-start | bytes 6291464 | tf_op jit(solution)/shard_map/ppermute | solution.py:348
  240.5 47.9 %collective-permute-start.21 = (f32[256,2048]{1,0:T(8,128)}, f32[256,2048]{1,0:T(8,128)}, u32[]{:S(2)}, u32[]{:S(2)}) collective-permute-start(f32[256,2048]{1,0:T(8,128)} %copy-done.3), channel_id=1, source_target_pairs={{0,4},{4,0},{8,12},{12,8},{16,20},{20,16},{24,28},{28,24},{1,5},{5... | collective-permute-start | bytes 6291464 | tf_op jit(solution)/shard_map/ppermute | solution.py:348
  241.1 40.9 %collective-permute-start.24 = (f32[128,2048]{1,0:T(8,128)}, f32[128,2048]{1,0:T(8,128)}, u32[]{:S(2)}, u32[]{:S(2)}) collective-permute-start(f32[128,2048]{1,0:T(8,128)} %copy-done.5), channel_id=1, source_target_pairs={{0,4},{4,0},{8,12},{12,8},{16,20},{20,16},{24,28},{28,24},{1,5},{5... | collective-permute-start | bytes 3145736 | tf_op jit(solution)/shard_map/ppermute | solution.py:348
  255.5 32.9 %collective-permute-start.22 = (f32[128,2048]{1,0:T(8,128)}, f32[128,2048]{1,0:T(8,128)}, u32[]{:S(2)}, u32[]{:S(2)}) collective-permute-start(f32[128,2048]{1,0:T(8,128)} %copy-done.6), channel_id=1, source_target_pairs={{0,4},{4,0},{8,12},{12,8},{16,20},{20,16},{24,28},{28,24},{1,5},{5... | collective-permute-start | bytes 3145736 | tf_op jit(solution)/shard_map/ppermute | solution.py:348
  255.7 30.6 %collective-permute-start.20 = (f32[4,4,16,512]{3,2,1,0:T(8,128)S(1)}, f32[4,4,16,512]{3,2,1,0:T(8,128)}, u32[]{:S(2)}, u32[]{:S(2)}) collective-permute-start(f32[4,4,16,512]{3,2,1,0:T(8,128)S(1)} %pad_maximum_fusion.7), channel_id=1, source_target_pairs={{0,8},{4,12},{8,0},{12,4},{16,24},{20,28},{24,16},{28,20},{1,9},{5... | collective-permute-start | bytes 1572872 | tf_op jit(solution)/shard_map/ppermute | solution.py:348
  384.3 33.6 %collective-permute-start.29 = (f32[4,2,16,1024]{3,2,1,0:T(8,128)}, f32[4,2,16,1024]{3,2,1,0:T(8,128)S(1)}, u32[]{:S(2)}, u32[]{:S(2)}) collective-permute-start(f32[4,2,16,1024]{3,2,1,0:T(8,128)} %encode_all.2.refs_5_), channel_id=1, source_target_pairs={{0,8},{4,12},{8,0},{12,4},{16,24},{20,28},{24,16},{28,20},{1,9},{5... | collective-permute-start | bytes 1572872 | tf_op jit(solution)/shard_map/ppermute | solution.py:348
  553.0 23.2 %collective-permute-start.42 = (f32[4,128,256]{2,1,0:T(8,128)}, f32[4,128,256]{2,1,0:T(8,128)S(1)}, u32[]{:S(2)}, u32[]{:S(2)}) collective-permute-start(f32[4,128,256]{2,1,0:T(8,128)} %decode.6.refs_9_.refs_0_), channel_id=1, source_target_pairs={{0,8},{4,12},{8,0},{12,4},{16,24},{20,28},{24,16},{28,20},{1,9},{5... | collective-permute-start | bytes 1572872 | tf_op jit(solution)/shard_map/ppermute | solution.py:348
  596.0 23.5 %collective-permute-start.68 = (f32[4,128,256]{2,1,0:T(8,128)S(1)}, f32[4,128,256]{2,1,0:T(8,128)S(1)}, u32[]{:S(2)}, u32[]{:S(2)}) collective-permute-start(f32[4,128,256]{2,1,0:T(8,128)S(1)} %collective-permute-done.44.refs_11_.refs_2_), channel_id=1, source_target_pairs={{0,4},{4,0},{8,12},{12,8},{16,20},{20,16},{24,28},{28,24},{1,5},{5... | collective-permute-start | bytes 1572872 | tf_op jit(solution)/shard_map/ppermute | solution.py:348
  596.4 24.7 %collective-permute-start.64 = (f32[4,128,256]{2,1,0:T(8,128)S(1)}, f32[4,128,256]{2,1,0:T(8,128)S(1)}, u32[]{:S(2)}, u32[]{:S(2)}) collective-permute-start(f32[4,128,256]{2,1,0:T(8,128)S(1)} %collective-permute-done.43.refs_10_.refs_2_), channel_id=1, source_target_pairs={{0,8},{4,12},{8,0},{12,4},{16,24},{20,28},{24,16},{28,20},{1,9},{5... | collective-permute-start | bytes 1572872 | tf_op jit(solution)/shard_map/ppermute | solution.py:348
  596.8 24.2 %collective-permute-start.62 = (f32[4,128,256]{2,1,0:T(8,128)S(1)}, f32[4,128,256]{2,1,0:T(8,128)S(1)}, u32[]{:S(2)}, u32[]{:S(2)}) collective-permute-start(f32[4,128,256]{2,1,0:T(8,128)S(1)} %collective-permute-done.61.refs_1_), channel_id=1, source_target_pairs={{0,4},{4,0},{8,12},{12,8},{16,20},{20,16},{24,28},{28,24},{1,5},{5... | collective-permute-start | bytes 1572872 | tf_op jit(solution)/shard_map/ppermute | solution.py:348
  621.7 23.8 %collective-permute-start.49 = (f32[4,128,256]{2,1,0:T(8,128)}, f32[4,128,256]{2,1,0:T(8,128)S(1)}, u32[]{:S(2)}, u32[]{:S(2)}) collective-permute-start(f32[4,128,256]{2,1,0:T(8,128)} %decode.9.refs_0_), channel_id=1, source_target_pairs={{0,16},{4,20},{8,24},{12,28},{16,0},{20,4},{24,8},{28,12},{1,17},{... | collective-permute-start | bytes 1572872 | tf_op jit(solution)/shard_map/ppermute | solution.py:348
  656.0 27.5 %collective-permute-start.46 = (f32[4,128,256]{2,1,0:T(8,128)}, f32[4,128,256]{2,1,0:T(8,128)}, u32[]{:S(2)}, u32[]{:S(2)}) collective-permute-start(f32[4,128,256]{2,1,0:T(8,128)} %decode.9.refs_0_), channel_id=1, source_target_pairs={{0,4},{4,0},{8,12},{12,8},{16,20},{20,16},{24,28},{28,24},{1,5},{5... | collective-permute-start | bytes 1572872 | tf_op jit(solution)/shard_map/ppermute | solution.py:348
  656.6 27.0 %collective-permute-start.50 = (f32[4,128,256]{2,1,0:T(8,128)S(1)}, f32[4,128,256]{2,1,0:T(8,128)}, u32[]{:S(2)}, u32[]{:S(2)}) collective-permute-start(f32[4,128,256]{2,1,0:T(8,128)S(1)} %collective-permute-done.49.refs_2_), channel_id=1, source_target_pairs={{0,4},{4,0},{8,12},{12,8},{16,20},{20,16},{24,28},{28,24},{1,5},{5... | collective-permute-start | bytes 1572872 | tf_op jit(solution)/shard_map/ppermute | solution.py:348
  656.7 26.9 %collective-permute-start.48 = (f32[4,128,256]{2,1,0:T(8,128)}, f32[4,128,256]{2,1,0:T(8,128)}, u32[]{:S(2)}, u32[]{:S(2)}) collective-permute-start(f32[4,128,256]{2,1,0:T(8,128)} %collective-permute-done.47.refs_1_), channel_id=1, source_target_pairs={{0,4},{4,0},{8,12},{12,8},{16,20},{20,16},{24,28},{28,24},{1,5},{5... | collective-permute-start | bytes 1572872 | tf_op jit(solution)/shard_map/ppermute | solution.py:348
  (81 other events, 1460.3 us)

commit v2 on v1

--- a/solution.py
+++ b/solution.py
@@ -21,7 +21,7 @@
 
 
 def cost(flops, nbytes):
-    return pl.CostEstimate(flops=flops // 16, bytes_accessed=nbytes // 16, transcendentals=0)
+    return pl.CostEstimate(flops=flops, bytes_accessed=nbytes, transcendentals=0)
 
 
 def split(x):
@@ -103,7 +103,7 @@
             pltpu.VMEM((3 * cwidth, points), bf16),
             pltpu.VMEM((size, points), f32),
         ],
-        cost(6 * size * count * vrows * cwidth * points, 4 * size * count * vrows * cwidth),
+        cost(size * count * vrows * cwidth * points // 4, size * count * vrows * cwidth // 4),
         (at, x, c, v),
         after,
     )
@@ -209,14 +209,14 @@
     )
 
 
-def decode_kernel(part, start, factor, at_ref, y_ref, hi_ref, lo_ref, v_ref, ve_ref, ce_ref, *refs):
-    block_ref, o_ref, whole = refs[0], refs[-2], refs[-1]
+def decode_kernel(part, start, factor, stage, at_ref, y_ref, hi_ref, lo_ref, v_ref, ve_ref, ce_ref, *refs):
+    o_ref, whole = refs[-2:]
     batch, vrows, cwidth = o_ref.shape
     tiles, tile = y_ref.shape[0], y_ref.shape[3]
 
     @pl.when(pl.program_id(0) == 0)
     def _():
-        o_ref[...] = jnp.zeros_like(o_ref)
+        o_ref[...] = refs[0][...] if stage else jnp.zeros_like(o_ref)
 
     for e in range(tiles):
         if tiles == 1:
@@ -232,77 +232,91 @@
         got = dot(hi, chi, across) + dot(hi, clo, across) + dot(lo, chi, across)
         o_ref[i * part : (i + 1) * part] += got.reshape(part, vrows, cwidth)
 
-    @pl.when(pl.program_id(0) == pl.num_programs(0) - 1)
-    def _():
-        shifted = (ce_ref[...] - ve_ref[...]) - center_shift
-        result = factor * (o_ref[...] + shifted[None] * block_ref[...])
-        if len(refs) > 3:
-            result = result - refs[1][...]
-        o_ref[...] = result
+    if factor is not None:
+
+        @pl.when(pl.program_id(0) == pl.num_programs(0) - 1)
+        def _():
+            shifted = (ce_ref[...] - ve_ref[...]) - center_shift
+            result = factor * (o_ref[...] + shifted[None] * refs[stage][...])
+            if len(refs) > 3 + stage:
+                result = result - refs[stage + 1][...]
+            o_ref[...] = result
 
 
 def decode(y, chi, clo, v, ve, ce, at, amplitudes, first, chunk, chunks, factor, after):
-    tiles, pieces, size, tile = y.shape
+    tiles, pieces, size, tile = y[0].shape
     points = tiles * tile
     batch = size // chunks
     vrows, cwidth = v.shape[1], chi.shape[1]
     own = pl.BlockSpec((batch, vrows, cwidth), lambda p, at: (at[0] * chunks + chunk, 0, at[1]))
     mine = pl.BlockSpec((batch, vrows, cwidth), lambda p, at: (chunk, 0, 0))
+    fixed = pl.BlockSpec((batch, vrows, cwidth), lambda p, at: (0, 0, 0))
     blocks = [amplitudes] if first is None else [first, amplitudes]
-    return call(
-        functools.partial(decode_kernel, part_of(batch, vrows), chunk * batch, factor),
-        "decode",
-        (pieces,),
-        [
-            pl.BlockSpec((tiles, 1, size, tile), lambda p, at: (0, p, 0, 0)),
-            pl.BlockSpec((1, cwidth, points), lambda p, at: (p, 0, 0)),
-            pl.BlockSpec((1, cwidth, points), lambda p, at: (p, 0, 0)),
-            pl.BlockSpec((1, vrows, points), lambda p, at: (p, 0, 0)),
-            pl.BlockSpec((vrows, 1), lambda p, at: (0, 0)),
-            pl.BlockSpec((1, cwidth), lambda p, at: (0, at[1])),
-        ]
-        + ([own] if first is None else [mine, own]),
-        pl.BlockSpec((batch, vrows, cwidth), lambda p, at: (0, 0, 0)),
-        jax.ShapeDtypeStruct((batch, vrows, cwidth), f32),
-        [pltpu.VMEM((size, points), f32)],
-        cost(6 * batch * vrows * cwidth * points * pieces, 4 * (cwidth + vrows) * points * pieces),
-        (at, y, chi, clo, v, ve, ce, *blocks),
-        after,
-    )
-
-
-def place_kernel(c_ref, v_ref, *refs):
-    hi_ref, lo_ref, o_ref = refs[-3:]
+    total = None
+    for stage in range(len(y)):
+        last = stage == len(y) - 1
+
+        def piece(p, at, stage=stage):
+            return (stage * pieces + p, 0, 0)
+
+        total = call(
+            functools.partial(
+                decode_kernel, part_of(batch, vrows), chunk * batch, factor if last else None, stage
+            ),
+            "decode",
+            (pieces,),
+            [
+                pl.BlockSpec((tiles, 1, size, tile), lambda p, at: (0, p, 0, 0)),
+                pl.BlockSpec((1, cwidth, points), piece),
+                pl.BlockSpec((1, cwidth, points), piece),
+                pl.BlockSpec((1, vrows, points), piece),
+                pl.BlockSpec((vrows, 1), lambda p, at: (0, 0)),
+                pl.BlockSpec((1, cwidth), lambda p, at: (0, at[1])),
+            ]
+            + [fixed] * stage
+            + (([own] if first is None else [mine, own]) if last else []),
+            fixed,
+            jax.ShapeDtypeStruct((batch, vrows, cwidth), f32),
+            [pltpu.VMEM((size, points), f32)],
+            cost(6 * batch * vrows * cwidth * points * pieces, 4 * (cwidth + vrows) * points * pieces),
+            (at, y[stage], chi, clo, v, ve, ce, *([total] * stage), *(blocks if last else [])),
+            after,
+        )
+        after = ()
+    return total
+
+
+def place_kernel(c_ref, *refs):
+    hi_ref, lo_ref, mark_ref = refs[-3:]
     hi, lo = split(c_ref[...])
     hi_ref[0] = hi
     lo_ref[0] = lo
-    o_ref[0] = v_ref[...]
-
-
-def place(piece, vpiece, slot, so_far, n):
+    mark_ref[...] = jnp.zeros_like(mark_ref)
+
+
+def place(piece, slot, so_far, n):
     cwidth, points = piece.shape
-    vrows = vpiece.shape[0]
-    tile = min(points, 512)
+    tile = min(points, 1024)
     carried = [] if so_far is None else list(so_far)
-    rows = [cwidth, cwidth, vrows]
-    return pl.pallas_call(
+    shape = jax.ShapeDtypeStruct((n, cwidth, points), bf16)
+    out = pl.BlockSpec((1, cwidth, tile), lambda j: (slot, 0, j))
+    *placed, mark = pl.pallas_call(
         place_kernel,
         grid=(points // tile,),
-        in_specs=[pl.BlockSpec((r, tile), lambda j: (0, j)) for r in rows[1:]]
-        + [anywhere] * len(carried),
-        out_specs=[pl.BlockSpec((1, r, tile), lambda j: (slot, 0, j)) for r in rows],
-        out_shape=[
-            jax.ShapeDtypeStruct((n, r, points), t) for r, t in zip(rows, (bf16, bf16, f32))
-        ],
-        input_output_aliases={2 + i: i for i in range(len(carried))},
+        in_specs=[pl.BlockSpec((cwidth, tile), lambda j: (0, j))] + [anywhere] * len(carried),
+        out_specs=[out, out, pl.BlockSpec((8, 128), lambda j: (0, 0))],
+        out_shape=[shape, shape, jax.ShapeDtypeStruct((8, 128), f32)],
+        input_output_aliases={1 + i: i for i in range(len(carried))},
         compiler_params=params(),
-        cost_estimate=cost(0, 8 * (cwidth + vrows) * points),
+        cost_estimate=cost(0, 16 * cwidth * points),
         name="place",
-    )(piece, vpiece, *carried)
+    )(piece, *carried)
+    return placed, mark
 
 
 def put_kernel(owners, chunk, chunks, count, at_ref, *refs):
-    pieces, out, held, came, went = refs[:count], refs[-4], refs[-3], refs[-2], refs[-1]
+    pieces, (out, mark, held, came, went) = refs[:count], refs[-5:]
+    mark[...] = jnp.zeros_like(mark)
     batch, _, cwidth = pieces[0].shape
     arriving = [pltpu.make_async_copy(pieces[i], held.at[i], came.at[i]) for i in range(count)]
     for copy in arriving:
@@ -330,8 +344,8 @@
     return pl.pallas_call(
         functools.partial(put_kernel, owners, chunk, chunks, count),
         in_specs=[pl.BlockSpec(memory_space=pltpu.SMEM)] + [anywhere] * (count + len(carried)),
-        out_specs=anywhere,
-        out_shape=jax.ShapeDtypeStruct(shape, f32),
+        out_specs=[anywhere, pl.BlockSpec(memory_space=pltpu.VMEM)],
+        out_shape=[jax.ShapeDtypeStruct(shape, f32), jax.ShapeDtypeStruct((8, 128), f32)],
         scratch_shapes=[
             pltpu.VMEM((count,) + block, f32),
             pltpu.SemaphoreType.DMA((count,)),
@@ -339,7 +353,7 @@
         ],
         input_output_aliases={count + 1 + i: i for i in range(len(carried))},
         compiler_params=params(),
-        cost_estimate=cost(0, 8 * count * pieces[owners[0]].size),
+        cost_estimate=cost(0, 16 * count * pieces[owners[0]].size),
         name="put",
     )(at, *[pieces[d] for d in owners], *carried)
 
@@ -371,21 +385,9 @@
 
 
 def scatter_sum(x, axis, size):
-    for bit in reversed(bits_of(size)):
-        sent = flip(x[bit:], axis, bit, size)
-        x = x[:bit] + sent
+    for bit in bits_of(size):
+        x = take_bit(x, 0, 1, 0) + flip(take_bit(x, 0, 1, 1), axis, bit, size)
     return x[0]
-
-
-def collect(x, axis, size, order):
-    x = x[None]
-    got = {0: x[0]}
-    done = []
-    for bit in order:
-        for d in list(got):
-            got[d | bit] = flip(got[d], axis, bit, size)
-        done.append(bit)
-    return [got[d] for d in range(size)]
 
 
 class Comm:
@@ -408,25 +410,79 @@
     return [2] + [b for b in bits_of(n) if b >= 4] + [1]
 
 
-def spread_encoded(x, comm):
+def join_kernel(a_ref, b_ref, *refs):
+    o_ref = refs[-1]
+    o_ref[0] = a_ref[...]
+    o_ref[1] = b_ref[...]
+
+
+def join(a, b, after):
+    whole = pl.BlockSpec(memory_space=pltpu.VMEM)
+    out = pl.pallas_call(
+        join_kernel,
+        in_specs=[whole, whole] + [anywhere] * len(after),
+        out_specs=whole,
+        out_shape=jax.ShapeDtypeStruct((2,) + a.shape, f32),
+        compiler_params=params(),
+        cost_estimate=cost(0, 16 * a.size),
+        name="join",
+    )(a, b, *after)
+    return out.reshape((2 * a.shape[0],) + a.shape[1:])
+
+
+def spread_encoded(x, comm, after=()):
     x = x[None]
-    for bit in spread_bits(comm.n):
-        x = jnp.concatenate([x, flip(x, "pts", bit, comm.n)], axis=0)
+    for i, bit in enumerate(spread_bits(comm.n)):
+        other = flip(x, "pts", bit, comm.n)
+        x = join(x, other, after) if after and i == 0 else jnp.concatenate([x, other], axis=0)
     return x
 
 
-def send_encoded_own(x, comm):
-    n, no, per = comm.n, comm.no, comm.per
+def arrange_kernel(at_ref, x_ref, v_ref, o_ref, copy_ref):
+    no, per = o_ref.shape[:2]
+    for e in range(no):
+        for c in range(per):
+            o_ref[e, c] = x_ref[((e ^ at_ref[3]) * per + c) ^ at_ref[2]]
+    copy_ref[...] = v_ref[...]
+
+
+def arrange(x, v, at, no, after):
+    n, batch, width = x.shape
+    per = n // no
+    return call(
+        arrange_kernel,
+        "arrange",
+        (1,),
+        [
+            pl.BlockSpec((n, batch, width), lambda i, at: (0, 0, 0)),
+            pl.BlockSpec(v.shape, lambda i, at: (0, 0)),
+        ],
+        [
+            pl.BlockSpec((no, per, batch, width), lambda i, at: (0, 0, 0, 0)),
+            pl.BlockSpec(v.shape, lambda i, at: (0, 0)),
+        ],
+        [jax.ShapeDtypeStruct((no, per, batch, width), f32), jax.ShapeDtypeStruct(v.shape, f32)],
+        [],
+        cost(0, 8 * x.size),
+        (at, x, v),
+        after,
+    )
+
+
+def send_encoded_own(x, v, at, comm, after):
+    n, no = comm.n, comm.no
     x = x[None]
     for bit in bits_of(n):
         dim = 1 if bit == 2 else 2
         other = flip(take_bit(x, dim, 1, 1), "pts", bit, n)
         x = jnp.concatenate([take_bit(x, dim, 1, 0), other], axis=0)
-    x = x[:, 0, 0].reshape((no, per) + x.shape[3:])
-    x = reorder(x, 0, (comm.me // per) ^ comm.mo)
-    if per > 1:
-        x = reorder(x, 1, comm.me % per)
-    return spread_encoded(scatter_sum(x, "orb", no), comm)
+    x, v = arrange(x[:, 0, 0], v, at, no, after)
+    vpieces = {0: v}
+    for bit in [b for b in bits_of(n) if b >= 4] + [2]:
+        for d in list(vpieces):
+            vpieces[d | bit] = flip(vpieces[d], "pts", bit, n)
+    early = tuple(vpieces[b] for b in bits_of(n) if b >= 4)
+    return spread_encoded(scatter_sum(x, "orb", no), comm, early), vpieces
 
 
 def send_encoded_all(send, keep, comm):
@@ -434,30 +490,39 @@
     return spread_encoded(scatter_sum(x, "orb", comm.no), comm)
 
 
-def send_interacted(x, comm):
+def send_interacted(x, comm, before=None):
     n, no = comm.n, comm.no
     x = x[:, None]
     for bit in [b for b in bits_of(n) if b != 2]:
         other = flip(take_bit(x, 2, 1, 1), "pts", bit, n)
         x = jnp.concatenate([take_bit(x, 2, 1, 0), other], axis=1)
-    x = scatter_sum(x[:, :, 0], "orb", no)[None]
-    for bit in bits_of(no):
-        x = jnp.concatenate([x, flip(x, "orb", bit, no)], axis=0)
-    x = jnp.concatenate([x, flip(x, "pts", 2, n)], axis=1)
-    if x.shape[3] % 128 == 0:
-        return x
-    x = reorder(x, 0, comm.mo).transpose(1, 2, 0, 3)
-    return x.reshape((1,) + x.shape[:2] + (-1,))
+    x = x[:, :, 0]
+    if before is not None:
+        x = tie(x, before)
+    x = scatter_sum(x, "orb", no)[None]
+    near, far = {0: x}, {0: flip(x, "pts", 2, n)}
+    for bit in reversed(bits_of(no)):
+        have = sorted(near)
+        more = flip(jnp.concatenate([near[e] for e in have], axis=0), "orb", bit, no)
+        side = flip(more, "pts", 2, n)
+        for i, e in enumerate(have):
+            near[e | bit], far[e | bit] = more[i : i + 1], side[i : i + 1]
+    result = []
+    for side in (near, far):
+        x = jnp.concatenate([side[e] for e in range(no)], axis=0)
+        if x.shape[3] % 128:
+            x = reorder(x, 0, comm.mo).transpose(1, 2, 0, 3)
+            x = x.reshape((1,) + x.shape[:2] + (-1,))
+        result.append(x)
+    return result
 
 
 def around(x, order, n):
     got = {0: x}
-    stages = []
     for bit in order:
-        new = {d | bit: flip(got[d], "pts", bit, n) for d in list(got)}
-        got.update(new)
-        stages.append(new)
-    return got, stages
+        for d in list(got):
+            got[d | bit] = flip(got[d], "pts", bit, n)
+    return got
 
 
 def body(
@@ -474,45 +539,43 @@
     other = lax.dynamic_slice_in_dim(conduction_points, (1 - comm.half) * cwidth, cwidth, 0)
     high = [b for b in bits_of(n) if b >= 4]
 
-    pieces = {0: mine, 2: flip(other, "pts", 2, n)}
-    vpieces = {0: valence_points, high[0]: flip(valence_points, "pts", high[0], n)}
-    pieces[high[0]] = flip(mine, "pts", high[0], n)
+
+    pieces = {0: mine, 2: flip(other, "pts", 2, n), high[0]: flip(mine, "pts", high[0], n)}
     early = (pieces[2], pieces[high[0]])
+    cuts = [0, teams - teams // 4, teams]
     parts, after = [], ()
-    runs = 4 if teams % 4 == 0 else 1
-    for i in range(runs):
+    for start, end in zip(cuts, cuts[1:]):
         part = encode_own(
-            amplitudes,
-            conduction_points,
-            valence_points,
-            at,
-            i * (teams // runs),
-            teams // runs,
-            size,
-            after + (early if i == runs - 1 else ()),
+            amplitudes, conduction_points, valence_points, at, start, end - start, size, after
         )
-        after = (part,)
+        after = (part,) + early
         parts.append(part)
-    part = jnp.concatenate(parts, axis=1)
     for bit in high:
         for d in list(pieces):
             if d | bit not in pieces:
-                pieces[d | bit] = flip(pieces[d], "pts", bit, n)
-    for bit in high[1:] + [2]:
-        for d in list(vpieces):
-            vpieces[d | bit] = flip(vpieces[d], "pts", bit, n)
-    second = tuple(pieces[d] for d in pieces if d not in (0, 2, high[0]))
-    second += tuple(vpieces[d] for d in vpieces if d != 0)
-    e = send_encoded_own(part, comm)
-    got = interact(e, screened, at, after + second)
-
-    for d in list(pieces):
+                pieces[d | bit] = flip(tie(pieces[d], parts[0]), "pts", bit, n)
+    across_x = tuple(pieces[d] for d in pieces if d not in (0, 2, high[0]))
+    near = list(pieces)
+    placed, marks = None, []
+    for d in near:
+        placed, mark = place(pieces[d], slot_of(d, n), placed, n)
+        marks.append(mark)
         pieces[d | 1] = flip(pieces[d], "pts", 1, n)
+    e, vpieces = send_encoded_own(
+        jnp.concatenate(parts, axis=1),
+        valence_points,
+        at,
+        comm,
+        across_x + tuple(marks[: len(marks) - len(across_x)]),
+    )
+    got = interact(e, screened, at, after)
+    for d in near:
+        placed, _ = place(pieces[d | 1], slot_of(d | 1, n), placed, n)
+
+    for d in list(vpieces):
         vpieces[d | 1] = flip(vpieces[d], "pts", 1, n)
-    placed = None
-    for d in pieces:
-        placed = place(pieces[d], vpieces[d], slot_of(d, n), placed, n)
-    chi, clo, v = placed
+    v = jnp.stack([vpieces[d] for d in sorted(vpieces, key=lambda d: slot_of(d, n))])
+    chi, clo = placed
 
     def decoded(y, first, chunk, chunks, factor, after):
         return decode(y, chi, clo, v, ve, ce, at, amplitudes, first, chunk, chunks, factor, after)
@@ -523,20 +586,34 @@
     keep = encode_all(first, chi, clo, v, at, 0, n, no, (send,))
     e = send_encoded_all(send, keep, comm)
     y = send_interacted(interact(e, screened, at, ()), comm)
-    out, after = None, ()
-    waiting = []
+    out, after, marks = None, (), []
+    waiting, decodes = [], []
+    both = [jnp.concatenate(y, axis=1)]
     for chunk in range(chunks):
         if chunk >= 2:
-            after += tuple(waiting[chunk - 2][1][0].values())
+            after += tuple(waiting[chunk - 2][b] for b in high + [2])
         if chunk >= 3:
-            after += tuple(waiting[chunk - 3][1][-1].values())
-        got = decoded(y, first, chunk, chunks, 1.0, after)
+            after += tuple(waiting[chunk - 3].values())
+        got = decoded(y if chunk == 0 else both, first, chunk, chunks, 1.0, after)
         after = (got,)
+        decodes.append(got)
         waiting.append(around(got, [2] + high if chunk % 2 == 0 else high + [2], n))
-    for chunk, (near, _) in enumerate(waiting):
-        out = put(near, chunk, chunks, at, out, amplitudes.shape)
-        far = {d | 1: flip(near[d], "pts", 1, n) for d in near}
-        out = put(far, chunk, chunks, at, out, amplitudes.shape)
+    for chunk, blocks in enumerate(waiting):
+        for d in list(blocks):
+            block = blocks[d]
+            if chunk < chunks - 2:
+                block = tie(block, decodes[chunk + 2])
+            if chunk == chunks - 1:
+                block = tie(block, tuple(marks[: chunks - 2]))
+            blocks[d | 1] = flip(block, "pts", 1, n)
+        if chunk < chunks - 1:
+            out, mark = put(blocks, chunk, chunks, at, out, amplitudes.shape)
+            marks.append(mark)
+        else:
+            near = {d: blocks[d] for d in blocks if d % 2 == 0}
+            out, _ = put(near, chunk, chunks, at, out, amplitudes.shape)
+            far = {d: blocks[d] for d in blocks if d % 2 == 1}
+            out, _ = put(far, chunk, chunks, at, out, amplitudes.shape)
     return out
 
 

time: 697 us -> 612 us (0.88)
  waiting for transfers between devices: 258 us -> 153 us
  local copies, waits for them, and re-layouts: 13.2 us -> 28.4 us
  starting transfers between devices: 39.6 us -> 51.1 us
  Pallas kernels: 366 us -> 355 us
    ppermute x70 -> x74, waiting for transfers between devices: 258 us -> 153 us  [flip(): return lax.ppermute(x, axis, [(i, i ^ bit) for i in range(size)])]
    unnamed x74 -> x91, local copies, waits for them, and re-layouts: 4.79 us -> 18.5 us
    pallas_call x8, Pallas kernels: 33.4 us -> 21.8 us  [place(): pl.pallas_call(place_kernel, grid=(points // tile,), in_specs=[pl.BlockSp...]
    ppermute x70 -> x74, starting transfers between devices: 39.6 us -> 51.1 us  [flip(): return lax.ppermute(x, axis, [(i, i ^ bit) for i in range(size)])]
    pallas_call x8 -> x5, Pallas kernels: 24.7 us -> 22 us  [put(): pl.pallas_call(functools.partial(put_kernel, owners, chunk, chunks, count...]
    pallas_call x13 -> x14, Pallas kernels: 308 us -> 310 us  [call(): pl.pallas_call(run, grid_spec=pltpu.PrefetchScalarGridSpec(num_scalar_pre...]
  transfers between devices with their start and end apart: 70 -> 74, of which waited for: 32 -> 29; matrix products, arithmetic and copies ran while one was open for 1% -> 4% of each run, Pallas kernels for 28% -> 43%
where the time goes in v2:
time: 612 us; the launch traced here: 603 us
  Pallas kernels  355 us (58%)
  waiting for transfers between devices  153 us (25%)
  starting transfers between devices  51.1 us (8%)
  local copies, waits for them, and re-layouts  28.4 us (5%)
  other arithmetic  14.4 us (2%)
    pallas_call x14, Pallas kernels, call(): pl.pallas_call(run, grid_spec=pltpu.PrefetchScalarGridSpec(num_scalar_pre...  310 us
    ppermute x74, waiting for transfers between devices, flip(): return lax.ppermute(x, axis, [(i, i ^ bit) for i in range(size)])  153 us
    ppermute x74, starting transfers between devices, flip(): return lax.ppermute(x, axis, [(i, i ^ bit) for i in range(size)])  51.1 us
    pallas_call x5, Pallas kernels, put(): pl.pallas_call(functools.partial(put_kernel, owners, chunk, chunks, count...  22 us
    pallas_call x8, Pallas kernels, place(): pl.pallas_call(place_kernel, grid=(points // tile,), in_specs=[pl.BlockSp...  21.8 us
    unnamed x91, local copies, waits for them, and re-layouts  18.5 us
  transfers between devices with their start and end apart: 74, of which 29 were waited for; matrix products, arithmetic and copies ran while one was open for 4% of the time, Pallas kernels for 43%

profile of v2, /device:TPU:0, one launch (start us, length us, event | category | flops | bytes accessed | tf_op | source)
XLA Modules:
  0.0 603.1 jit_solution(9902533201250513317)
XLA Ops:
  9.8 45.5 %encode_own.2.refs_4_ = f32[2,3,16,1024]{3,2,1,0:T(8,128)} custom-call(s32[4]{0:T(128)} %pad_add_fusion.refs_0_.at_ref, f32[64,128,512]{2,1,0:T(8,128)} %refs_8_.7, f32[512,2048]{1,0:T(8,128)} %refs_2_.6, f32[128,2048]{1,0:T(8,128)} %refs_2_.7), custom_call_target="tpu_custom_call" | custom-call | flops 1610612736 | bytes 786432 | tf_op jit(solution)/shard_map/encode_own/pallas_call | solution.py:46
  57.2 18.2 %encode_own.3.refs_3_ = f32[2,1,16,1024]{3,2,1,0:T(8,128)} custom-call(s32[4]{0:T(128)} %pad_add_fusion.refs_0_.at_ref, f32[64,128,512]{2,1,0:T(8,128)} %refs_8_.7, f32[512,2048]{1,0:T(8,128)} %refs_2_.6, f32[128,2048]{1,0:T(8,128)} %refs_2_.7, f32[2,3,16,1024]{3,2,1,0:T(8,128)} %encode_own.2.refs_4_, ...), custom_call_target="tpu_custom_call" | custom-call | flops 536870912 | bytes 262144 | tf_op jit(solution)/shard_map/encode_own/pallas_call | solution.py:46
  79.1 7.3 %collective-permute-done.3 = f32[2,1,2,16,1024]{4,3,0,2,1:T(8,128)S(1)} collective-permute-done((f32[2,1,2,16,1024]{4,3,0,2,1:T(8,128)S(1)}, f32[2,1,2,16,1024]{4,3,0,2,1:T(8,128)S(1)}, u32[]{:S(2)}, u32[]{:S(2)}) %collective-permute-start.3) | collective-permute-done | bytes 262176 | tf_op jit(solution)/shard_map/ppermute | solution.py:362
  96.8 11.2 %collective-permute-done.4 = f32[4,1,1,16,1024]{4,3,0,2,1:T(8,128)S(1)} collective-permute-done((f32[4,1,1,16,1024]{4,3,0,2,1:T(8,128)S(1)}, f32[4,1,1,16,1024]{4,3,0,2,1:T(8,128)S(1)}, u32[]{:S(2)}, u32[]{:S(2)}) %collective-permute-start.4) | collective-permute-done | bytes 262176 | tf_op jit(solution)/shard_map/ppermute | solution.py:362
  145.0 7.7 %collective-permute-done.10 = f32[2,2,16,1024]{3,2,1,0:T(8,128)S(1)} collective-permute-done((f32[2,2,16,1024]{3,2,1,0:T(8,128)}, f32[2,2,16,1024]{3,2,1,0:T(8,128)S(1)}, u32[]{:S(2)}, u32[]{:S(2)}) %collective-permute-start.10) | collective-permute-done | bytes 262176 | tf_op jit(solution)/shard_map/ppermute | solution.py:362
  172.4 17.2 %interact.2 = f32[4,4,16,512]{3,2,1,0:T(8,128)} custom-call(s32[4]{0:T(128)} %pad_add_fusion.refs_0_.at_ref, f32[8,2,16,1024]{3,2,1,0:T(8,128)} %pad_maximum_fusion.refs_1_, f32[2048,4096]{1,0:T(8,128)} %refs_2_.9, f32[2,1,16,1024]{3,2,1,0:T(8,128)} %encode_own.3.refs_3_, f32[256,2048]{1,0:T(8,128)} %collective-permute-done.refs_5_.c_ref.refs_4_, ...), custom_call_target="tpu_custom_call" | custom-call | flops 3221225472 | bytes 33554432 | tf_op jit(solution)/shard_map/interact/pallas_call | solution.py:46
  202.8 6.2 %collective-permute-done.14 = f32[2,4,16,512]{3,2,1,0:T(8,128)S(1)} collective-permute-done((f32[2,4,16,512]{3,2,1,0:T(8,128)S(1)}, f32[2,4,16,512]{3,2,1,0:T(8,128)S(1)}, u32[]{:S(2)}, u32[]{:S(2)}) %collective-permute-start.14) | collective-permute-done | bytes 262176 | tf_op jit(solution)/shard_map/ppermute | solution.py:362
  233.8 31.1 %decode.7.refs_7_ = f32[16,128,256]{2,1,0:T(8,128)} custom-call(s32[4]{0:T(128)} %pad_add_fusion.refs_0_.at_ref, f32[4,4,16,512]{3,2,1,0:T(8,128)} %pad_maximum_fusion.5.refs_1_, bf16[8,256,2048]{2,1,0:T(8,128)(2,1)} %get-tuple-element.66.refs_2_, bf16[8,256,2048]{2,1,0:T(8,128)(2,1)} %get-tuple-element.67.refs_3_, ...), custom_call_target="tpu_custom_call" | custom-call | flops 25769803776 | bytes 12582912 | tf_op jit(solution)/shard_map/decode/pallas_call | solution.py:46
  265.7 33.2 %decode.8.refs_1_.refs_8_.refs_7_ = f32[16,128,256]{2,1,0:T(8,128)} custom-call(s32[4]{0:T(128)} %pad_add_fusion.refs_0_.at_ref, f32[4,4,16,512]{3,2,1,0:T(8,128)} %pad_maximum_fusion.4.refs_1_, bf16[8,256,2048]{2,1,0:T(8,128)(2,1)} %get-tuple-element.66.refs_2_, bf16[8,256,2048]{2,1,0:T(8,128)(2,1)} %get-tuple-element.67.refs_3_, ...), custom_call_target="tpu_custom_call" | custom-call | flops 25769803776 | bytes 12582912 | tf_op jit(solution)/shard_map/decode/pallas_call | solution.py:46
  299.0 32.1 %encode_all.2.refs_5_ = f32[4,2,16,1024]{3,2,1,0:T(8,128)} custom-call(s32[4]{0:T(128)} %pad_add_fusion.refs_0_.at_ref, f32[16,128,256]{2,1,0:T(8,128)} %decode.8.refs_1_.refs_8_.refs_7_, bf16[8,256,2048]{2,1,0:T(8,128)(2,1)} %get-tuple-element.66.refs_2_, bf16[8,256,2048]{2,1,0:T(8,128)(2,1)} %get-tuple-element.67.refs_3_, ...), custom_call_target="tpu_custom_call" | custom-call | flops 25769803776 | bytes 12582912 | tf_op jit(solution)/shard_map/encode_all/pallas_call | solution.py:46
  331.6 32.3 %encode_all.3 = f32[4,2,16,1024]{3,2,1,0:T(8,128)} custom-call(s32[4]{0:T(128)} %pad_add_fusion.refs_0_.at_ref, f32[16,128,256]{2,1,0:T(8,128)} %decode.8.refs_1_.refs_8_.refs_7_, bf16[8,256,2048]{2,1,0:T(8,128)(2,1)} %get-tuple-element.66.refs_2_, bf16[8,256,2048]{2,1,0:T(8,128)(2,1)} %get-tuple-element.67.refs_3_, ...), custom_call_target="tpu_custom_call" | custom-call | flops 25769803776 | bytes 12582912 | tf_op jit(solution)/shard_map/encode_all/pallas_call | solution.py:46
  365.1 7.8 %collective-permute-done.32 = f32[2,2,16,1024]{3,2,1,0:T(8,128)S(1)} collective-permute-done((f32[2,2,16,1024]{3,2,1,0:T(8,128)S(1)}, f32[2,2,16,1024]{3,2,1,0:T(8,128)S(1)}, u32[]{:S(2)}, u32[]{:S(2)}) %collective-permute-start.32) | collective-permute-done | bytes 262176 | tf_op jit(solution)/shard_map/ppermute | solution.py:362
  393.8 17.2 %interact.3 = f32[4,4,16,512]{3,2,1,0:T(8,128)} custom-call(s32[4]{0:T(128)} %pad_add_fusion.refs_0_.at_ref, f32[8,2,16,1024]{3,2,1,0:T(8,128)} %pad_maximum_fusion.1.refs_1_, f32[2048,4096]{1,0:T(8,128)} %refs_2_.9), custom_call_target="tpu_custom_call" | custom-call | flops 3221225472 | bytes 33554432 | tf_op jit(solution)/shard_map/interact/pallas_call | solution.py:46
  414.5 7.7 %collective-permute-done.38 = f32[4,2,1,16,512]{4,3,1,0,2:T(8,128)S(1)} collective-permute-done((f32[4,2,1,16,512]{4,3,1,0,2:T(8,128)S(1)}, f32[4,2,1,16,512]{4,3,1,0,2:T(8,128)S(1)}, u32[]{:S(2)}, u32[]{:S(2)}) %collective-permute-start.38) | collective-permute-done | bytes 262176 | tf_op jit(solution)/shard_map/ppermute | solution.py:362
  422.3 7.5 %collective-permute-done.39 = f32[2,4,16,512]{3,2,1,0:T(8,128)S(1)} collective-permute-done((f32[2,4,16,512]{3,2,1,0:T(8,128)S(1)}, f32[2,4,16,512]{3,2,1,0:T(8,128)S(1)}, u32[]{:S(2)}, u32[]{:S(2)}) %collective-permute-start.39) | collective-permute-done | bytes 262176 | tf_op jit(solution)/shard_map/ppermute | solution.py:362
  431.0 6.4 %collective-permute-done.40 = f32[1,4,16,512]{3,2,1,0:T(8,128)S(1)} collective-permute-done((f32[1,4,16,512]{3,2,1,0:T(8,128)S(1)}, f32[1,4,16,512]{3,2,1,0:T(8,128)S(1)}, u32[]{:S(2)}, u32[]{:S(2)}) %collective-permute-start.40) | collective-permute-done | bytes 131104 | tf_op jit(solution)/shard_map/ppermute | solution.py:362
  437.5 7.2 %collective-permute-done.41 = f32[1,4,16,512]{3,2,1,0:T(8,128)S(1)} collective-permute-done((f32[1,4,16,512]{3,2,1,0:T(8,128)S(1)}, f32[1,4,16,512]{3,2,1,0:T(8,128)S(1)}, u32[]{:S(2)}, u32[]{:S(2)}) %collective-permute-start.41) | collective-permute-done | bytes 131104 | tf_op jit(solution)/shard_map/ppermute | solution.py:362
  454.8 10.9 %decode.9.refs_7_ = f32[4,128,256]{2,1,0:T(8,128)} custom-call(s32[4]{0:T(128)} %pad_add_fusion.refs_0_.at_ref, f32[4,4,16,512]{3,2,1,0:T(8,128)} %pad_maximum_fusion.7.refs_1_, bf16[8,256,2048]{2,1,0:T(8,128)(2,1)} %get-tuple-element.66.refs_2_, bf16[8,256,2048]{2,1,0:T(8,128)(2,1)} %get-tuple-element.67.refs_3_, ...), custom_call_target="tpu_custom_call" | custom-call | flops 6442450944 | bytes 12582912 | tf_op jit(solution)/shard_map/decode/pallas_call | solution.py:46
  466.6 11.7 %decode.10.refs_9_.refs_12_.refs_0_ = f32[4,128,256]{2,1,0:T(8,128)} custom-call(s32[4]{0:T(128)} %pad_add_fusion.refs_0_.at_ref, f32[4,4,16,512]{3,2,1,0:T(8,128)} %pad_maximum_fusion.8.refs_1_, bf16[8,256,2048]{2,1,0:T(8,128)(2,1)} %get-tuple-element.66.refs_2_, bf16[8,256,2048]{2,1,0:T(8,128)(2,1)} %get-tuple-element.67.refs_3_, ...), custom_call_target="tpu_custom_call" | custom-call | flops 6442450944 | bytes 12582912 | tf_op jit(solution)/shard_map/decode/pallas_call | solution.py:46
  480.6 19.3 %decode.11.refs_9_.refs_0_ = f32[4,128,256]{2,1,0:T(8,128)} custom-call(s32[4]{0:T(128)} %pad_add_fusion.refs_0_.at_ref, f32[4,8,16,512]{3,2,1,0:T(8,128)} %maximum_maximum_fusion.refs_1_, bf16[8,256,2048]{2,1,0:T(8,128)(2,1)} %get-tuple-element.66.refs_2_, bf16[8,256,2048]{2,1,0:T(8,128)(2,1)} %get-tuple-element.67.refs_3_, ...), custom_call_target="tpu_custom_call" | custom-call | flops 12884901888 | bytes 25165824 | tf_op jit(solution)/shard_map/decode/pallas_call | solution.py:46
  504.3 19.0 %decode.12.refs_9_.refs_0_ = f32[4,128,256]{2,1,0:T(8,128)} custom-call(s32[4]{0:T(128)} %pad_add_fusion.refs_0_.at_ref, f32[4,8,16,512]{3,2,1,0:T(8,128)} %maximum_maximum_fusion.refs_1_, bf16[8,256,2048]{2,1,0:T(8,128)(2,1)} %get-tuple-element.66.refs_2_, bf16[8,256,2048]{2,1,0:T(8,128)(2,1)} %get-tuple-element.67.refs_3_, ...), custom_call_target="tpu_custom_call" | custom-call | flops 12884901888 | bytes 25165824 | tf_op jit(solution)/shard_map/decode/pallas_call | solution.py:46
  526.1 19.1 %decode.13.refs_0_ = f32[4,128,256]{2,1,0:T(8,128)} custom-call(s32[4]{0:T(128)} %pad_add_fusion.refs_0_.at_ref, f32[4,8,16,512]{3,2,1,0:T(8,128)} %maximum_maximum_fusion.refs_1_, bf16[8,256,2048]{2,1,0:T(8,128)(2,1)} %get-tuple-element.66.refs_2_, bf16[8,256,2048]{2,1,0:T(8,128)(2,1)} %get-tuple-element.67.refs_3_, ...), custom_call_target="tpu_custom_call" | custom-call | flops 12884901888 | bytes 25165824 | tf_op jit(solution)/shard_map/decode/pallas_call | solution.py:46
  547.9 12.1 %collective-permute-done.70.refs_4_ = f32[4,128,256]{2,1,0:T(8,128)S(1)} collective-permute-done((f32[4,128,256]{2,1,0:T(8,128)S(1)}, f32[4,128,256]{2,1,0:T(8,128)S(1)}, u32[]{:S(2)}, u32[]{:S(2)}) %collective-permute-start.70) | collective-permute-done | bytes 524320 | tf_op jit(solution)/shard_map/ppermute | solution.py:362
  562.5 8.7 %collective-permute-done.63.refs_2_ = f32[4,128,256]{2,1,0:T(8,128)S(1)} collective-permute-done((f32[4,128,256]{2,1,0:T(8,128)}, f32[4,128,256]{2,1,0:T(8,128)S(1)}, u32[]{:S(2)}, u32[]{:S(2)}) %collective-permute-start.63) | collective-permute-done | bytes 524320 | tf_op jit(solution)/shard_map/ppermute | solution.py:362
  (293 shorter events, 205.5 us)
Async XLA Ops:
  4.7 50.5 %collective-permute-start = (f32[256,2048]{1,0:T(8,128)}, f32[256,2048]{1,0:T(8,128)}, u32[]{:S(2)}, u32[]{:S(2)}) collective-permute-start(f32[256,2048]{1,0:T(8,128)} %get-tuple-element.88), channel_id=1, source_target_pairs={{0,8},{4,12},{8,0},{12,4},{16,24},{20,28},{24,16},{28,20},{1,9},{5... | collective-permute-start | bytes 6291464 | tf_op jit(solution)/shard_map/ppermute | solution.py:362
  7.7 48.2 %collective-permute-start.1 = (f32[256,2048]{1,0:T(8,128)}, f32[256,2048]{1,0:T(8,128)S(1)}, u32[]{:S(2)}, u32[]{:S(2)}) collective-permute-start(f32[256,2048]{1,0:T(8,128)} %get-tuple-element.87.c_ref), channel_id=1, source_target_pairs={{0,16},{4,20},{8,24},{12,28},{16,0},{20,4},{24,8},{28,12},{1,17},{... | collective-permute-start | bytes 6291464 | tf_op jit(solution)/shard_map/ppermute | solution.py:362
  55.3 53.6 %collective-permute-start.5 = (f32[256,2048]{1,0:T(8,128)}, f32[256,2048]{1,0:T(8,128)S(1)}, u32[]{:S(2)}, u32[]{:S(2)}) collective-permute-start(f32[256,2048]{1,0:T(8,128)} %collective-permute-done.refs_5_.c_ref.refs_4_), channel_id=1, source_target_pairs={{0,16},{4,20},{8,24},{12,28},{16,0},{20,4},{24,8},{28,12},{1,17},{... | collective-permute-start | bytes 6291464 | tf_op jit(solution)/shard_map/ppermute | solution.py:362
  88.1 67.1 %collective-permute-start.24 = (f32[256,2048]{1,0:T(8,128)}, f32[256,2048]{1,0:T(8,128)}, u32[]{:S(2)}, u32[]{:S(2)}) collective-permute-start(f32[256,2048]{1,0:T(8,128)} %get-tuple-element.87.c_ref), channel_id=1, source_target_pairs={{0,4},{4,0},{8,12},{12,8},{16,20},{20,16},{24,28},{28,24},{1,5},{5... | collective-permute-start | bytes 6291464 | tf_op jit(solution)/shard_map/ppermute | solution.py:362
  90.8 65.0 %collective-permute-start.23 = (f32[256,2048]{1,0:T(8,128)}, f32[256,2048]{1,0:T(8,128)}, u32[]{:S(2)}, u32[]{:S(2)}) collective-permute-start(f32[256,2048]{1,0:T(8,128)} %collective-permute-done.refs_5_.c_ref.refs_4_), channel_id=1, source_target_pairs={{0,4},{4,0},{8,12},{12,8},{16,20},{20,16},{24,28},{28,24},{1,5},{5... | collective-permute-start | bytes 6291464 | tf_op jit(solution)/shard_map/ppermute | solution.py:362
  116.0 50.4 %collective-permute-start.22 = (f32[256,2048]{1,0:T(8,128)S(1)}, f32[256,2048]{1,0:T(8,128)}, u32[]{:S(2)}, u32[]{:S(2)}) collective-permute-start(f32[256,2048]{1,0:T(8,128)S(1)} %copy-done.1), channel_id=1, source_target_pairs={{0,4},{4,0},{8,12},{12,8},{16,20},{20,16},{24,28},{28,24},{1,5},{5... | collective-permute-start | bytes 6291464 | tf_op jit(solution)/shard_map/ppermute | solution.py:362
  116.0 25.8 %collective-permute-start.9 = (f32[128,2048]{1,0:T(8,128)}, f32[128,2048]{1,0:T(8,128)S(1)}, u32[]{:S(2)}, u32[]{:S(2)}) collective-permute-start(f32[128,2048]{1,0:T(8,128)} %get-tuple-element.55), channel_id=1, source_target_pairs={{0,16},{4,20},{8,24},{12,28},{16,0},{20,4},{24,8},{28,12},{1,17},{... | collective-permute-start | bytes 3145736 | tf_op jit(solution)/shard_map/ppermute | solution.py:362
  135.8 33.9 %collective-permute-start.27 = (f32[128,2048]{1,0:T(8,128)}, f32[128,2048]{1,0:T(8,128)}, u32[]{:S(2)}, u32[]{:S(2)}) collective-permute-start(f32[128,2048]{1,0:T(8,128)} %get-tuple-element.55), channel_id=1, source_target_pairs={{0,8},{4,12},{8,0},{12,4},{16,24},{20,28},{24,16},{28,20},{1,9},{5... | collective-permute-start | bytes 3145736 | tf_op jit(solution)/shard_map/ppermute | solution.py:362
  155.3 35.4 %collective-permute-start.25 = (f32[128,2048]{1,0:T(8,128)}, f32[128,2048]{1,0:T(8,128)S(1)}, u32[]{:S(2)}, u32[]{:S(2)}) collective-permute-start(f32[128,2048]{1,0:T(8,128)} %get-tuple-element.55), channel_id=1, source_target_pairs={{0,4},{4,0},{8,12},{12,8},{16,20},{20,16},{24,28},{28,24},{1,5},{5... | collective-permute-start | bytes 3145736 | tf_op jit(solution)/shard_map/ppermute | solution.py:362
  155.8 38.6 %collective-permute-start.21 = (f32[256,2048]{1,0:T(8,128)}, f32[256,2048]{1,0:T(8,128)S(1)}, u32[]{:S(2)}, u32[]{:S(2)}) collective-permute-start(f32[256,2048]{1,0:T(8,128)} %copy-done.2), channel_id=1, source_target_pairs={{0,4},{4,0},{8,12},{12,8},{16,20},{20,16},{24,28},{28,24},{1,5},{5... | collective-permute-start | bytes 6291464 | tf_op jit(solution)/shard_map/ppermute | solution.py:362
  169.2 32.5 %collective-permute-start.26 = (f32[128,2048]{1,0:T(8,128)S(1)}, f32[128,2048]{1,0:T(8,128)S(1)}, u32[]{:S(2)}, u32[]{:S(2)}) collective-permute-start(f32[128,2048]{1,0:T(8,128)S(1)} %copy-done.5), channel_id=1, source_target_pairs={{0,4},{4,0},{8,12},{12,8},{16,20},{20,16},{24,28},{28,24},{1,5},{5... | collective-permute-start | bytes 3145736 | tf_op jit(solution)/shard_map/ppermute | solution.py:362
  169.7 44.4 %collective-permute-start.29 = (f32[128,2048]{1,0:T(8,128)S(1)}, f32[128,2048]{1,0:T(8,128)S(1)}, u32[]{:S(2)}, u32[]{:S(2)}) collective-permute-start(f32[128,2048]{1,0:T(8,128)S(1)} %copy-done.5), channel_id=1, source_target_pairs={{0,8},{4,12},{8,0},{12,4},{16,24},{20,28},{24,16},{28,20},{1,9},{5... | collective-permute-start | bytes 3145736 | tf_op jit(solution)/shard_map/ppermute | solution.py:362
  170.2 47.6 %collective-permute-start.28 = (f32[128,2048]{1,0:T(8,128)}, f32[128,2048]{1,0:T(8,128)S(1)}, u32[]{:S(2)}, u32[]{:S(2)}) collective-permute-start(f32[128,2048]{1,0:T(8,128)} %collective-permute-done.27), channel_id=1, source_target_pairs={{0,4},{4,0},{8,12},{12,8},{16,20},{20,16},{24,28},{28,24},{1,5},{5... | collective-permute-start | bytes 3145736 | tf_op jit(solution)/shard_map/ppermute | solution.py:362
  225.1 39.7 %collective-permute-start.16 = (f32[1,4,16,512]{3,2,1,0:T(8,128)S(1)}, f32[1,4,16,512]{3,2,1,0:T(8,128)S(1)}, u32[]{:S(2)}, u32[]{:S(2)}) collective-permute-start(f32[1,4,16,512]{3,2,1,0:T(8,128)S(1)} %fusion.16), channel_id=1, source_target_pairs={{0,8},{4,12},{8,0},{12,4},{16,24},{20,28},{24,16},{28,20},{1,9},{5... | collective-permute-start | bytes 393224 | tf_op jit(solution)/shard_map/ppermute | solution.py:362
  226.6 38.2 %collective-permute-start.20 = (f32[1,4,16,512]{3,2,1,0:T(8,128)S(1)}, f32[1,4,16,512]{3,2,1,0:T(8,128)S(1)}, u32[]{:S(2)}, u32[]{:S(2)}) collective-permute-start(f32[1,4,16,512]{3,2,1,0:T(8,128)S(1)} %collective-permute-done.17), channel_id=1, source_target_pairs={{0,8},{4,12},{8,0},{12,4},{16,24},{20,28},{24,16},{28,20},{1,9},{5... | collective-permute-start | bytes 393224 | tf_op jit(solution)/shard_map/ppermute | solution.py:362
  230.3 34.5 %collective-permute-start.19 = (f32[2,4,16,512]{3,2,1,0:T(8,128)S(1)}, f32[2,4,16,512]{3,2,1,0:T(8,128)S(1)}, u32[]{:S(2)}, u32[]{:S(2)}) collective-permute-start(f32[2,4,16,512]{3,2,1,0:T(8,128)S(1)} %collective-permute-done.18), channel_id=1, source_target_pairs={{0,8},{4,12},{8,0},{12,4},{16,24},{20,28},{24,16},{28,20},{1,9},{5... | collective-permute-start | bytes 786440 | tf_op jit(solution)/shard_map/ppermute | solution.py:362
  331.0 32.8 %collective-permute-start.31 = (f32[4,2,16,1024]{3,2,1,0:T(8,128)}, f32[4,2,16,1024]{3,2,1,0:T(8,128)S(1)}, u32[]{:S(2)}, u32[]{:S(2)}) collective-permute-start(f32[4,2,16,1024]{3,2,1,0:T(8,128)} %encode_all.2.refs_5_), channel_id=1, source_target_pairs={{0,8},{4,12},{8,0},{12,4},{16,24},{20,28},{24,16},{28,20},{1,9},{5... | collective-permute-start | bytes 1572872 | tf_op jit(solution)/shard_map/ppermute | solution.py:362
  478.3 24.9 %collective-permute-start.46 = (f32[4,128,256]{2,1,0:T(8,128)}, f32[4,128,256]{2,1,0:T(8,128)S(1)}, u32[]{:S(2)}, u32[]{:S(2)}) collective-permute-start(f32[4,128,256]{2,1,0:T(8,128)} %decode.10.refs_9_.refs_12_.refs_0_), channel_id=1, source_target_pairs={{0,16},{4,20},{8,24},{12,28},{16,0},{20,4},{24,8},{28,12},{1,17},{... | collective-permute-start | bytes 1572872 | tf_op jit(solution)/shard_map/ppermute | solution.py:362
  478.8 23.9 %collective-permute-start.47 = (f32[4,128,256]{2,1,0:T(8,128)}, f32[4,128,256]{2,1,0:T(8,128)S(1)}, u32[]{:S(2)}, u32[]{:S(2)}) collective-permute-start(f32[4,128,256]{2,1,0:T(8,128)} %decode.10.refs_9_.refs_12_.refs_0_), channel_id=1, source_target_pairs={{0,8},{4,12},{8,0},{12,4},{16,24},{20,28},{24,16},{28,20},{1,9},{5... | collective-permute-start | bytes 1572872 | tf_op jit(solution)/shard_map/ppermute | solution.py:362
  499.9 24.1 %collective-permute-start.48 = (f32[4,128,256]{2,1,0:T(8,128)}, f32[4,128,256]{2,1,0:T(8,128)S(1)}, u32[]{:S(2)}, u32[]{:S(2)}) collective-permute-start(f32[4,128,256]{2,1,0:T(8,128)} %decode.11.refs_9_.refs_0_), channel_id=1, source_target_pairs={{0,16},{4,20},{8,24},{12,28},{16,0},{20,4},{24,8},{28,12},{1,17},{... | collective-permute-start | bytes 1572872 | tf_op jit(solution)/shard_map/ppermute | solution.py:362
  501.2 23.3 %collective-permute-start.49 = (f32[4,128,256]{2,1,0:T(8,128)}, f32[4,128,256]{2,1,0:T(8,128)S(1)}, u32[]{:S(2)}, u32[]{:S(2)}) collective-permute-start(f32[4,128,256]{2,1,0:T(8,128)} %decode.11.refs_9_.refs_0_), channel_id=1, source_target_pairs={{0,8},{4,12},{8,0},{12,4},{16,24},{20,28},{24,16},{28,20},{1,9},{5... | collective-permute-start | bytes 1572872 | tf_op jit(solution)/shard_map/ppermute | solution.py:362
  523.4 23.7 %collective-permute-start.68 = (f32[4,128,256]{2,1,0:T(8,128)}, f32[4,128,256]{2,1,0:T(8,128)S(1)}, u32[]{:S(2)}, u32[]{:S(2)}) collective-permute-start(f32[4,128,256]{2,1,0:T(8,128)} %decode.12.refs_9_.refs_0_), channel_id=1, source_target_pairs={{0,8},{4,12},{8,0},{12,4},{16,24},{20,28},{24,16},{28,20},{1,9},{5... | collective-permute-start | bytes 1572872 | tf_op jit(solution)/shard_map/ppermute | solution.py:362
  547.1 24.1 %collective-permute-start.63 = (f32[4,128,256]{2,1,0:T(8,128)}, f32[4,128,256]{2,1,0:T(8,128)S(1)}, u32[]{:S(2)}, u32[]{:S(2)}) collective-permute-start(f32[4,128,256]{2,1,0:T(8,128)} %decode.13.refs_0_), channel_id=1, source_target_pairs={{0,16},{4,20},{8,24},{12,28},{16,0},{20,4},{24,8},{28,12},{1,17},{... | collective-permute-start | bytes 1572872 | tf_op jit(solution)/shard_map/ppermute | solution.py:362
  561.3 24.1 %collective-permute-start.72 = (f32[4,128,256]{2,1,0:T(8,128)S(1)}, f32[4,128,256]{2,1,0:T(8,128)S(1)}, u32[]{:S(2)}, u32[]{:S(2)}) collective-permute-start(f32[4,128,256]{2,1,0:T(8,128)S(1)} %collective-permute-done.68.refs_2_), channel_id=1, source_target_pairs={{0,16},{4,20},{8,24},{12,28},{16,0},{20,4},{24,8},{28,12},{1,17},{... | collective-permute-start | bytes 1572872 | tf_op jit(solution)/shard_map/ppermute | solution.py:362
  (90 other events, 1060.7 us)

commit v3 on v2

--- a/solution.py
+++ b/solution.py
@@ -518,10 +518,11 @@
 
 
 def around(x, order, n):
-    got = {0: x}
-    for bit in order:
+    own = {bit: flip(x, "pts", bit, n) for bit in order}
+    got = {0: x, order[0]: tie(own[order[0]], tuple(own.values()))}
+    for bit in order[1:]:
         for d in list(got):
-            got[d | bit] = flip(got[d], "pts", bit, n)
+            got[d | bit] = own[bit] if d == 0 else flip(got[d], "pts", bit, n)
     return got
 
 

time: 612 us -> 601 us (0.982)
  waiting for transfers between devices: 153 us -> 141 us
    ppermute x74, waiting for transfers between devices: 153 us -> 141 us  [flip(): return lax.ppermute(x, axis, [(i, i ^ bit) for i in range(size)])]
    unnamed x91 -> x97, local copies, waits for them, and re-layouts: 18.5 us -> 20.2 us
where the time goes in v3:
time: 601 us; the launch traced here: 593 us
  Pallas kernels  355 us (59%)
  waiting for transfers between devices  141 us (23%)
  starting transfers between devices  49.9 us (8%)
  local copies, waits for them, and re-layouts  30.2 us (5%)
  other arithmetic  14.5 us (2%)
    pallas_call x14, Pallas kernels, call(): pl.pallas_call(run, grid_spec=pltpu.PrefetchScalarGridSpec(num_scalar_pre...  310 us
    ppermute x74, waiting for transfers between devices, flip(): return lax.ppermute(x, axis, [(i, i ^ bit) for i in range(size)])  141 us
    ppermute x74, starting transfers between devices, flip(): return lax.ppermute(x, axis, [(i, i ^ bit) for i in range(size)])  49.9 us
    pallas_call x5, Pallas kernels, put(): pl.pallas_call(functools.partial(put_kernel, owners, chunk, chunks, count...  22 us
    pallas_call x8, Pallas kernels, place(): pl.pallas_call(place_kernel, grid=(points // tile,), in_specs=[pl.BlockSp...  21.9 us
    unnamed x97, local copies, waits for them, and re-layouts  20.2 us
  transfers between devices with their start and end apart: 74, of which 29 were waited for; matrix products, arithmetic and copies ran while one was open for 4% of the time, Pallas kernels for 43%

profile of v3, /device:TPU:0, one launch (start us, length us, event | category | flops | bytes accessed | tf_op | source)
XLA Modules:
  0.0 592.5 jit_solution(8989765356753284779)
XLA Ops:
  9.8 45.5 %encode_own.2.refs_4_ = f32[2,3,16,1024]{3,2,1,0:T(8,128)} custom-call(s32[4]{0:T(128)} %pad_add_fusion.refs_0_.at_ref, f32[64,128,512]{2,1,0:T(8,128)} %refs_8_.7, f32[512,2048]{1,0:T(8,128)} %refs_2_.6, f32[128,2048]{1,0:T(8,128)} %refs_2_.7), custom_call_target="tpu_custom_call" | custom-call | flops 1610612736 | bytes 786432 | tf_op jit(solution)/shard_map/encode_own/pallas_call | solution.py:46
  57.2 18.2 %encode_own.3.refs_3_ = f32[2,1,16,1024]{3,2,1,0:T(8,128)} custom-call(s32[4]{0:T(128)} %pad_add_fusion.refs_0_.at_ref, f32[64,128,512]{2,1,0:T(8,128)} %refs_8_.7, f32[512,2048]{1,0:T(8,128)} %refs_2_.6, f32[128,2048]{1,0:T(8,128)} %refs_2_.7, f32[2,3,16,1024]{3,2,1,0:T(8,128)} %encode_own.2.refs_4_, ...), custom_call_target="tpu_custom_call" | custom-call | flops 536870912 | bytes 262144 | tf_op jit(solution)/shard_map/encode_own/pallas_call | solution.py:46
  79.2 7.4 %collective-permute-done.3 = f32[2,1,2,16,1024]{4,3,0,2,1:T(8,128)S(1)} collective-permute-done((f32[2,1,2,16,1024]{4,3,0,2,1:T(8,128)S(1)}, f32[2,1,2,16,1024]{4,3,0,2,1:T(8,128)S(1)}, u32[]{:S(2)}, u32[]{:S(2)}) %collective-permute-start.3) | collective-permute-done | bytes 262176 | tf_op jit(solution)/shard_map/ppermute | solution.py:362
  97.0 11.1 %collective-permute-done.4 = f32[4,1,1,16,1024]{4,3,0,2,1:T(8,128)S(1)} collective-permute-done((f32[4,1,1,16,1024]{4,3,0,2,1:T(8,128)S(1)}, f32[4,1,1,16,1024]{4,3,0,2,1:T(8,128)S(1)}, u32[]{:S(2)}, u32[]{:S(2)}) %collective-permute-start.4) | collective-permute-done | bytes 262176 | tf_op jit(solution)/shard_map/ppermute | solution.py:362
  130.1 5.7 collective-permute-done.8.b_ref
  145.1 7.7 %collective-permute-done.10 = f32[2,2,16,1024]{3,2,1,0:T(8,128)S(1)} collective-permute-done((f32[2,2,16,1024]{3,2,1,0:T(8,128)}, f32[2,2,16,1024]{3,2,1,0:T(8,128)S(1)}, u32[]{:S(2)}, u32[]{:S(2)}) %collective-permute-start.10) | collective-permute-done | bytes 262176 | tf_op jit(solution)/shard_map/ppermute | solution.py:362
  172.5 17.2 %interact.2 = f32[4,4,16,512]{3,2,1,0:T(8,128)} custom-call(s32[4]{0:T(128)} %pad_add_fusion.refs_0_.at_ref, f32[8,2,16,1024]{3,2,1,0:T(8,128)} %pad_maximum_fusion.refs_1_, f32[2048,4096]{1,0:T(8,128)} %refs_2_.9, f32[2,1,16,1024]{3,2,1,0:T(8,128)} %encode_own.3.refs_3_, f32[256,2048]{1,0:T(8,128)} %collective-permute-done.refs_5_.c_ref.refs_4_, ...), custom_call_target="tpu_custom_call" | custom-call | flops 3221225472 | bytes 33554432 | tf_op jit(solution)/shard_map/interact/pallas_call | solution.py:46
  202.9 6.2 %collective-permute-done.14 = f32[2,4,16,512]{3,2,1,0:T(8,128)S(1)} collective-permute-done((f32[2,4,16,512]{3,2,1,0:T(8,128)S(1)}, f32[2,4,16,512]{3,2,1,0:T(8,128)S(1)}, u32[]{:S(2)}, u32[]{:S(2)}) %collective-permute-start.14) | collective-permute-done | bytes 262176 | tf_op jit(solution)/shard_map/ppermute | solution.py:362
  233.9 31.1 %decode.7.refs_7_ = f32[16,128,256]{2,1,0:T(8,128)} custom-call(s32[4]{0:T(128)} %pad_add_fusion.refs_0_.at_ref, f32[4,4,16,512]{3,2,1,0:T(8,128)} %pad_maximum_fusion.5.refs_1_, bf16[8,256,2048]{2,1,0:T(8,128)(2,1)} %get-tuple-element.70.refs_2_, bf16[8,256,2048]{2,1,0:T(8,128)(2,1)} %get-tuple-element.71.refs_3_, ...), custom_call_target="tpu_custom_call" | custom-call | flops 25769803776 | bytes 12582912 | tf_op jit(solution)/shard_map/decode/pallas_call | solution.py:46
  265.9 33.2 %decode.8.refs_1_.refs_8_.refs_7_ = f32[16,128,256]{2,1,0:T(8,128)} custom-call(s32[4]{0:T(128)} %pad_add_fusion.refs_0_.at_ref, f32[4,4,16,512]{3,2,1,0:T(8,128)} %pad_maximum_fusion.4.refs_1_, bf16[8,256,2048]{2,1,0:T(8,128)(2,1)} %get-tuple-element.70.refs_2_, bf16[8,256,2048]{2,1,0:T(8,128)(2,1)} %get-tuple-element.71.refs_3_, ...), custom_call_target="tpu_custom_call" | custom-call | flops 25769803776 | bytes 12582912 | tf_op jit(solution)/shard_map/decode/pallas_call | solution.py:46
  299.1 32.1 %encode_all.2.refs_5_ = f32[4,2,16,1024]{3,2,1,0:T(8,128)} custom-call(s32[4]{0:T(128)} %pad_add_fusion.refs_0_.at_ref, f32[16,128,256]{2,1,0:T(8,128)} %decode.8.refs_1_.refs_8_.refs_7_, bf16[8,256,2048]{2,1,0:T(8,128)(2,1)} %get-tuple-element.70.refs_2_, bf16[8,256,2048]{2,1,0:T(8,128)(2,1)} %get-tuple-element.71.refs_3_, ...), custom_call_target="tpu_custom_call" | custom-call | flops 25769803776 | bytes 12582912 | tf_op jit(solution)/shard_map/encode_all/pallas_call | solution.py:46
  331.7 32.3 %encode_all.3 = f32[4,2,16,1024]{3,2,1,0:T(8,128)} custom-call(s32[4]{0:T(128)} %pad_add_fusion.refs_0_.at_ref, f32[16,128,256]{2,1,0:T(8,128)} %decode.8.refs_1_.refs_8_.refs_7_, bf16[8,256,2048]{2,1,0:T(8,128)(2,1)} %get-tuple-element.70.refs_2_, bf16[8,256,2048]{2,1,0:T(8,128)(2,1)} %get-tuple-element.71.refs_3_, ...), custom_call_target="tpu_custom_call" | custom-call | flops 25769803776 | bytes 12582912 | tf_op jit(solution)/shard_map/encode_all/pallas_call | solution.py:46
  365.2 7.8 %collective-permute-done.32 = f32[2,2,16,1024]{3,2,1,0:T(8,128)S(1)} collective-permute-done((f32[2,2,16,1024]{3,2,1,0:T(8,128)S(1)}, f32[2,2,16,1024]{3,2,1,0:T(8,128)S(1)}, u32[]{:S(2)}, u32[]{:S(2)}) %collective-permute-start.32) | collective-permute-done | bytes 262176 | tf_op jit(solution)/shard_map/ppermute | solution.py:362
  393.9 17.2 %interact.3 = f32[4,4,16,512]{3,2,1,0:T(8,128)} custom-call(s32[4]{0:T(128)} %pad_add_fusion.refs_0_.at_ref, f32[8,2,16,1024]{3,2,1,0:T(8,128)} %pad_maximum_fusion.1.refs_1_, f32[2048,4096]{1,0:T(8,128)} %refs_2_.9), custom_call_target="tpu_custom_call" | custom-call | flops 3221225472 | bytes 33554432 | tf_op jit(solution)/shard_map/interact/pallas_call | solution.py:46
  414.6 7.7 %collective-permute-done.38 = f32[4,2,1,16,512]{4,3,1,0,2:T(8,128)S(1)} collective-permute-done((f32[4,2,1,16,512]{4,3,1,0,2:T(8,128)S(1)}, f32[4,2,1,16,512]{4,3,1,0,2:T(8,128)S(1)}, u32[]{:S(2)}, u32[]{:S(2)}) %collective-permute-start.38) | collective-permute-done | bytes 262176 | tf_op jit(solution)/shard_map/ppermute | solution.py:362
  422.5 7.5 %collective-permute-done.39 = f32[2,4,16,512]{3,2,1,0:T(8,128)S(1)} collective-permute-done((f32[2,4,16,512]{3,2,1,0:T(8,128)S(1)}, f32[2,4,16,512]{3,2,1,0:T(8,128)S(1)}, u32[]{:S(2)}, u32[]{:S(2)}) %collective-permute-start.39) | collective-permute-done | bytes 262176 | tf_op jit(solution)/shard_map/ppermute | solution.py:362
  431.1 6.5 %collective-permute-done.40 = f32[1,4,16,512]{3,2,1,0:T(8,128)S(1)} collective-permute-done((f32[1,4,16,512]{3,2,1,0:T(8,128)S(1)}, f32[1,4,16,512]{3,2,1,0:T(8,128)S(1)}, u32[]{:S(2)}, u32[]{:S(2)}) %collective-permute-start.40) | collective-permute-done | bytes 131104 | tf_op jit(solution)/shard_map/ppermute | solution.py:362
  437.7 7.2 %collective-permute-done.41 = f32[1,4,16,512]{3,2,1,0:T(8,128)S(1)} collective-permute-done((f32[1,4,16,512]{3,2,1,0:T(8,128)S(1)}, f32[1,4,16,512]{3,2,1,0:T(8,128)S(1)}, u32[]{:S(2)}, u32[]{:S(2)}) %collective-permute-start.41) | collective-permute-done | bytes 131104 | tf_op jit(solution)/shard_map/ppermute | solution.py:362
  455.0 10.9 %decode.9.refs_7_ = f32[4,128,256]{2,1,0:T(8,128)} custom-call(s32[4]{0:T(128)} %pad_add_fusion.refs_0_.at_ref, f32[4,4,16,512]{3,2,1,0:T(8,128)} %pad_maximum_fusion.7.refs_1_, bf16[8,256,2048]{2,1,0:T(8,128)(2,1)} %get-tuple-element.70.refs_2_, bf16[8,256,2048]{2,1,0:T(8,128)(2,1)} %get-tuple-element.71.refs_3_, ...), custom_call_target="tpu_custom_call" | custom-call | flops 6442450944 | bytes 12582912 | tf_op jit(solution)/shard_map/decode/pallas_call | solution.py:46
  466.8 11.6 %decode.10.refs_9_.refs_12_.refs_0_ = f32[4,128,256]{2,1,0:T(8,128)} custom-call(s32[4]{0:T(128)} %pad_add_fusion.refs_0_.at_ref, f32[4,4,16,512]{3,2,1,0:T(8,128)} %pad_maximum_fusion.8.refs_1_, bf16[8,256,2048]{2,1,0:T(8,128)(2,1)} %get-tuple-element.70.refs_2_, bf16[8,256,2048]{2,1,0:T(8,128)(2,1)} %get-tuple-element.71.refs_3_, ...), custom_call_target="tpu_custom_call" | custom-call | flops 6442450944 | bytes 12582912 | tf_op jit(solution)/shard_map/decode/pallas_call | solution.py:46
  480.7 19.3 %decode.11.refs_9_.refs_0_ = f32[4,128,256]{2,1,0:T(8,128)} custom-call(s32[4]{0:T(128)} %pad_add_fusion.refs_0_.at_ref, f32[4,8,16,512]{3,2,1,0:T(8,128)} %maximum_maximum_fusion.refs_1_, bf16[8,256,2048]{2,1,0:T(8,128)(2,1)} %get-tuple-element.70.refs_2_, bf16[8,256,2048]{2,1,0:T(8,128)(2,1)} %get-tuple-element.71.refs_3_, ...), custom_call_target="tpu_custom_call" | custom-call | flops 12884901888 | bytes 25165824 | tf_op jit(solution)/shard_map/decode/pallas_call | solution.py:46
  503.9 19.0 %decode.12.refs_9_.refs_0_ = f32[4,128,256]{2,1,0:T(8,128)} custom-call(s32[4]{0:T(128)} %pad_add_fusion.refs_0_.at_ref, f32[4,8,16,512]{3,2,1,0:T(8,128)} %maximum_maximum_fusion.refs_1_, bf16[8,256,2048]{2,1,0:T(8,128)(2,1)} %get-tuple-element.70.refs_2_, bf16[8,256,2048]{2,1,0:T(8,128)(2,1)} %get-tuple-element.71.refs_3_, ...), custom_call_target="tpu_custom_call" | custom-call | flops 12884901888 | bytes 25165824 | tf_op jit(solution)/shard_map/decode/pallas_call | solution.py:46
  526.7 19.1 %decode.13.refs_0_ = f32[4,128,256]{2,1,0:T(8,128)} custom-call(s32[4]{0:T(128)} %pad_add_fusion.refs_0_.at_ref, f32[4,8,16,512]{3,2,1,0:T(8,128)} %maximum_maximum_fusion.refs_1_, bf16[8,256,2048]{2,1,0:T(8,128)(2,1)} %get-tuple-element.70.refs_2_, bf16[8,256,2048]{2,1,0:T(8,128)(2,1)} %get-tuple-element.71.refs_3_, ...), custom_call_target="tpu_custom_call" | custom-call | flops 12884901888 | bytes 25165824 | tf_op jit(solution)/shard_map/decode/pallas_call | solution.py:46
  549.8 10.3 %collective-permute-done.61.refs_1_ = f32[4,128,256]{2,1,0:T(8,128)S(1)} collective-permute-done((f32[4,128,256]{2,1,0:T(8,128)}, f32[4,128,256]{2,1,0:T(8,128)S(1)}, u32[]{:S(2)}, u32[]{:S(2)}) %collective-permute-start.61) | collective-permute-done | bytes 524320 | tf_op jit(solution)/shard_map/ppermute | solution.py:362
  (299 shorter events, 199.7 us)
Async XLA Ops:
  4.7 50.6 %collective-permute-start = (f32[256,2048]{1,0:T(8,128)}, f32[256,2048]{1,0:T(8,128)}, u32[]{:S(2)}, u32[]{:S(2)}) collective-permute-start(f32[256,2048]{1,0:T(8,128)} %get-tuple-element.96), channel_id=1, source_target_pairs={{0,8},{4,12},{8,0},{12,4},{16,24},{20,28},{24,16},{28,20},{1,9},{5... | collective-permute-start | bytes 6291464 | tf_op jit(solution)/shard_map/ppermute | solution.py:362
  7.7 48.2 %collective-permute-start.1 = (f32[256,2048]{1,0:T(8,128)}, f32[256,2048]{1,0:T(8,128)S(1)}, u32[]{:S(2)}, u32[]{:S(2)}) collective-permute-start(f32[256,2048]{1,0:T(8,128)} %get-tuple-element.95.c_ref), channel_id=1, source_target_pairs={{0,16},{4,20},{8,24},{12,28},{16,0},{20,4},{24,8},{28,12},{1,17},{... | collective-permute-start | bytes 6291464 | tf_op jit(solution)/shard_map/ppermute | solution.py:362
  55.3 53.6 %collective-permute-start.5 = (f32[256,2048]{1,0:T(8,128)}, f32[256,2048]{1,0:T(8,128)S(1)}, u32[]{:S(2)}, u32[]{:S(2)}) collective-permute-start(f32[256,2048]{1,0:T(8,128)} %collective-permute-done.refs_5_.c_ref.refs_4_), channel_id=1, source_target_pairs={{0,16},{4,20},{8,24},{12,28},{16,0},{20,4},{24,8},{28,12},{1,17},{... | collective-permute-start | bytes 6291464 | tf_op jit(solution)/shard_map/ppermute | solution.py:362
  88.2 67.2 %collective-permute-start.24 = (f32[256,2048]{1,0:T(8,128)}, f32[256,2048]{1,0:T(8,128)}, u32[]{:S(2)}, u32[]{:S(2)}) collective-permute-start(f32[256,2048]{1,0:T(8,128)} %get-tuple-element.95.c_ref), channel_id=1, source_target_pairs={{0,4},{4,0},{8,12},{12,8},{16,20},{20,16},{24,28},{28,24},{1,5},{5... | collective-permute-start | bytes 6291464 | tf_op jit(solution)/shard_map/ppermute | solution.py:362
  90.9 65.0 %collective-permute-start.23 = (f32[256,2048]{1,0:T(8,128)}, f32[256,2048]{1,0:T(8,128)}, u32[]{:S(2)}, u32[]{:S(2)}) collective-permute-start(f32[256,2048]{1,0:T(8,128)} %collective-permute-done.refs_5_.c_ref.refs_4_), channel_id=1, source_target_pairs={{0,4},{4,0},{8,12},{12,8},{16,20},{20,16},{24,28},{28,24},{1,5},{5... | collective-permute-start | bytes 6291464 | tf_op jit(solution)/shard_map/ppermute | solution.py:362
  116.1 50.5 %collective-permute-start.22 = (f32[256,2048]{1,0:T(8,128)S(1)}, f32[256,2048]{1,0:T(8,128)}, u32[]{:S(2)}, u32[]{:S(2)}) collective-permute-start(f32[256,2048]{1,0:T(8,128)S(1)} %copy-done.1), channel_id=1, source_target_pairs={{0,4},{4,0},{8,12},{12,8},{16,20},{20,16},{24,28},{28,24},{1,5},{5... | collective-permute-start | bytes 6291464 | tf_op jit(solution)/shard_map/ppermute | solution.py:362
  116.1 25.8 %collective-permute-start.9 = (f32[128,2048]{1,0:T(8,128)}, f32[128,2048]{1,0:T(8,128)S(1)}, u32[]{:S(2)}, u32[]{:S(2)}) collective-permute-start(f32[128,2048]{1,0:T(8,128)} %get-tuple-element.59), channel_id=1, source_target_pairs={{0,16},{4,20},{8,24},{12,28},{16,0},{20,4},{24,8},{28,12},{1,17},{... | collective-permute-start | bytes 3145736 | tf_op jit(solution)/shard_map/ppermute | solution.py:362
  135.8 33.9 %collective-permute-start.27 = (f32[128,2048]{1,0:T(8,128)}, f32[128,2048]{1,0:T(8,128)}, u32[]{:S(2)}, u32[]{:S(2)}) collective-permute-start(f32[128,2048]{1,0:T(8,128)} %get-tuple-element.59), channel_id=1, source_target_pairs={{0,8},{4,12},{8,0},{12,4},{16,24},{20,28},{24,16},{28,20},{1,9},{5... | collective-permute-start | bytes 3145736 | tf_op jit(solution)/shard_map/ppermute | solution.py:362
  155.3 35.4 %collective-permute-start.25 = (f32[128,2048]{1,0:T(8,128)}, f32[128,2048]{1,0:T(8,128)S(1)}, u32[]{:S(2)}, u32[]{:S(2)}) collective-permute-start(f32[128,2048]{1,0:T(8,128)} %get-tuple-element.59), channel_id=1, source_target_pairs={{0,4},{4,0},{8,12},{12,8},{16,20},{20,16},{24,28},{28,24},{1,5},{5... | collective-permute-start | bytes 3145736 | tf_op jit(solution)/shard_map/ppermute | solution.py:362
  155.9 38.6 %collective-permute-start.21 = (f32[256,2048]{1,0:T(8,128)}, f32[256,2048]{1,0:T(8,128)S(1)}, u32[]{:S(2)}, u32[]{:S(2)}) collective-permute-start(f32[256,2048]{1,0:T(8,128)} %copy-done.2), channel_id=1, source_target_pairs={{0,4},{4,0},{8,12},{12,8},{16,20},{20,16},{24,28},{28,24},{1,5},{5... | collective-permute-start | bytes 6291464 | tf_op jit(solution)/shard_map/ppermute | solution.py:362
  169.3 32.5 %collective-permute-start.26 = (f32[128,2048]{1,0:T(8,128)S(1)}, f32[128,2048]{1,0:T(8,128)S(1)}, u32[]{:S(2)}, u32[]{:S(2)}) collective-permute-start(f32[128,2048]{1,0:T(8,128)S(1)} %copy-done.5), channel_id=1, source_target_pairs={{0,4},{4,0},{8,12},{12,8},{16,20},{20,16},{24,28},{28,24},{1,5},{5... | collective-permute-start | bytes 3145736 | tf_op jit(solution)/shard_map/ppermute | solution.py:362
  169.8 44.4 %collective-permute-start.29 = (f32[128,2048]{1,0:T(8,128)S(1)}, f32[128,2048]{1,0:T(8,128)S(1)}, u32[]{:S(2)}, u32[]{:S(2)}) collective-permute-start(f32[128,2048]{1,0:T(8,128)S(1)} %copy-done.5), channel_id=1, source_target_pairs={{0,8},{4,12},{8,0},{12,4},{16,24},{20,28},{24,16},{28,20},{1,9},{5... | collective-permute-start | bytes 3145736 | tf_op jit(solution)/shard_map/ppermute | solution.py:362
  170.3 47.6 %collective-permute-start.28 = (f32[128,2048]{1,0:T(8,128)}, f32[128,2048]{1,0:T(8,128)S(1)}, u32[]{:S(2)}, u32[]{:S(2)}) collective-permute-start(f32[128,2048]{1,0:T(8,128)} %collective-permute-done.27), channel_id=1, source_target_pairs={{0,4},{4,0},{8,12},{12,8},{16,20},{20,16},{24,28},{28,24},{1,5},{5... | collective-permute-start | bytes 3145736 | tf_op jit(solution)/shard_map/ppermute | solution.py:362
  225.2 39.8 %collective-permute-start.16 = (f32[1,4,16,512]{3,2,1,0:T(8,128)S(1)}, f32[1,4,16,512]{3,2,1,0:T(8,128)S(1)}, u32[]{:S(2)}, u32[]{:S(2)}) collective-permute-start(f32[1,4,16,512]{3,2,1,0:T(8,128)S(1)} %fusion.16), channel_id=1, source_target_pairs={{0,8},{4,12},{8,0},{12,4},{16,24},{20,28},{24,16},{28,20},{1,9},{5... | collective-permute-start | bytes 393224 | tf_op jit(solution)/shard_map/ppermute | solution.py:362
  226.7 38.3 %collective-permute-start.20 = (f32[1,4,16,512]{3,2,1,0:T(8,128)S(1)}, f32[1,4,16,512]{3,2,1,0:T(8,128)S(1)}, u32[]{:S(2)}, u32[]{:S(2)}) collective-permute-start(f32[1,4,16,512]{3,2,1,0:T(8,128)S(1)} %collective-permute-done.17), channel_id=1, source_target_pairs={{0,8},{4,12},{8,0},{12,4},{16,24},{20,28},{24,16},{28,20},{1,9},{5... | collective-permute-start | bytes 393224 | tf_op jit(solution)/shard_map/ppermute | solution.py:362
  230.4 34.5 %collective-permute-start.19 = (f32[2,4,16,512]{3,2,1,0:T(8,128)S(1)}, f32[2,4,16,512]{3,2,1,0:T(8,128)S(1)}, u32[]{:S(2)}, u32[]{:S(2)}) collective-permute-start(f32[2,4,16,512]{3,2,1,0:T(8,128)S(1)} %collective-permute-done.18), channel_id=1, source_target_pairs={{0,8},{4,12},{8,0},{12,4},{16,24},{20,28},{24,16},{28,20},{1,9},{5... | collective-permute-start | bytes 786440 | tf_op jit(solution)/shard_map/ppermute | solution.py:362
  331.2 32.8 %collective-permute-start.31 = (f32[4,2,16,1024]{3,2,1,0:T(8,128)}, f32[4,2,16,1024]{3,2,1,0:T(8,128)S(1)}, u32[]{:S(2)}, u32[]{:S(2)}) collective-permute-start(f32[4,2,16,1024]{3,2,1,0:T(8,128)} %encode_all.2.refs_5_), channel_id=1, source_target_pairs={{0,8},{4,12},{8,0},{12,4},{16,24},{20,28},{24,16},{28,20},{1,9},{5... | collective-permute-start | bytes 1572872 | tf_op jit(solution)/shard_map/ppermute | solution.py:362
  478.4 24.4 %collective-permute-start.46 = (f32[4,128,256]{2,1,0:T(8,128)}, f32[4,128,256]{2,1,0:T(8,128)S(1)}, u32[]{:S(2)}, u32[]{:S(2)}) collective-permute-start(f32[4,128,256]{2,1,0:T(8,128)} %decode.10.refs_9_.refs_12_.refs_0_), channel_id=1, source_target_pairs={{0,16},{4,20},{8,24},{12,28},{16,0},{20,4},{24,8},{28,12},{1,17},{... | collective-permute-start | bytes 1572872 | tf_op jit(solution)/shard_map/ppermute | solution.py:362
  478.9 23.9 %collective-permute-start.47 = (f32[4,128,256]{2,1,0:T(8,128)}, f32[4,128,256]{2,1,0:T(8,128)S(1)}, u32[]{:S(2)}, u32[]{:S(2)}) collective-permute-start(f32[4,128,256]{2,1,0:T(8,128)} %decode.10.refs_9_.refs_12_.refs_0_), channel_id=1, source_target_pairs={{0,8},{4,12},{8,0},{12,4},{16,24},{20,28},{24,16},{28,20},{1,9},{5... | collective-permute-start | bytes 1572872 | tf_op jit(solution)/shard_map/ppermute | solution.py:362
  500.0 23.7 %collective-permute-start.48 = (f32[4,128,256]{2,1,0:T(8,128)}, f32[4,128,256]{2,1,0:T(8,128)S(1)}, u32[]{:S(2)}, u32[]{:S(2)}) collective-permute-start(f32[4,128,256]{2,1,0:T(8,128)} %decode.11.refs_9_.refs_0_), channel_id=1, source_target_pairs={{0,16},{4,20},{8,24},{12,28},{16,0},{20,4},{24,8},{28,12},{1,17},{... | collective-permute-start | bytes 1572872 | tf_op jit(solution)/shard_map/ppermute | solution.py:362
  501.3 23.3 %collective-permute-start.49 = (f32[4,128,256]{2,1,0:T(8,128)}, f32[4,128,256]{2,1,0:T(8,128)S(1)}, u32[]{:S(2)}, u32[]{:S(2)}) collective-permute-start(f32[4,128,256]{2,1,0:T(8,128)} %decode.11.refs_9_.refs_0_), channel_id=1, source_target_pairs={{0,8},{4,12},{8,0},{12,4},{16,24},{20,28},{24,16},{28,20},{1,9},{5... | collective-permute-start | bytes 1572872 | tf_op jit(solution)/shard_map/ppermute | solution.py:362
  523.0 26.1 %collective-permute-start.68 = (f32[4,128,256]{2,1,0:T(8,128)}, f32[4,128,256]{2,1,0:T(8,128)S(1)}, u32[]{:S(2)}, u32[]{:S(2)}) collective-permute-start(f32[4,128,256]{2,1,0:T(8,128)} %decode.12.refs_9_.refs_0_), channel_id=1, source_target_pairs={{0,8},{4,12},{8,0},{12,4},{16,24},{20,28},{24,16},{28,20},{1,9},{5... | collective-permute-start | bytes 1572872 | tf_op jit(solution)/shard_map/ppermute | solution.py:362
  523.6 26.1 %collective-permute-start.69 = (f32[4,128,256]{2,1,0:T(8,128)}, f32[4,128,256]{2,1,0:T(8,128)S(1)}, u32[]{:S(2)}, u32[]{:S(2)}) collective-permute-start(f32[4,128,256]{2,1,0:T(8,128)} %decode.12.refs_9_.refs_0_), channel_id=1, source_target_pairs={{0,16},{4,20},{8,24},{12,28},{16,0},{20,4},{24,8},{28,12},{1,17},{... | collective-permute-start | bytes 1572872 | tf_op jit(solution)/shard_map/ppermute | solution.py:362
  525.2 23.9 %collective-permute-start.58 = (f32[4,128,256]{2,1,0:T(8,128)S(1)}, f32[4,128,256]{2,1,0:T(8,128)S(1)}, u32[]{:S(2)}, u32[]{:S(2)}) collective-permute-start(f32[4,128,256]{2,1,0:T(8,128)S(1)} %collective-permute-done.48.refs_10_.refs_4_), channel_id=1, source_target_pairs={{0,8},{4,12},{8,0},{12,4},{16,24},{20,28},{24,16},{28,20},{1,9},{5... | collective-permute-start | bytes 1572872 | tf_op jit(solution)/shard_map/ppermute | solution.py:362
  (93 other events, 935.3 us)

commit v4 on v3

--- a/solution.py
+++ b/solution.py
@@ -203,7 +203,7 @@
         pl.BlockSpec((1, n // 2, size, tile), lambda i, at: (i, 0, 0, 0)),
         jax.ShapeDtypeStruct((no, n // 2, size, tile), f32),
         [pltpu.VMEM((batch, columns), f32), pltpu.VMEM((2 * batch, columns), bf16)],
-        cost(6 * batch * columns * rows, 4 * columns * rows),
+        cost(6 * batch * columns * rows // 16, columns * rows // 4),
         (at, e, s),
         after,
     )

time: 601 us -> 598 us (level)
    unnamed x97 -> x99, local copies, waits for them, and re-layouts: 20.2 us -> 17.5 us
  transfers between devices with their start and end apart: 74 -> 74, of which waited for: 29 -> 28; matrix products, arithmetic and copies ran while one was open for 4% -> 4% of each run, Pallas kernels for 43% -> 44%
where the time goes in v4:
time: 598 us; the launch traced here: 589 us
  Pallas kernels  356 us (60%)
  waiting for transfers between devices  140 us (23%)
  starting transfers between devices  50.3 us (8%)
  local copies, waits for them, and re-layouts  27.5 us (5%)
  other arithmetic  14.5 us (2%)
    pallas_call x14, Pallas kernels, call(): pl.pallas_call(run, grid_spec=pltpu.PrefetchScalarGridSpec(num_scalar_pre...  310 us
    ppermute x74, waiting for transfers between devices, flip(): return lax.ppermute(x, axis, [(i, i ^ bit) for i in range(size)])  140 us
    ppermute x74, starting transfers between devices, flip(): return lax.ppermute(x, axis, [(i, i ^ bit) for i in range(size)])  50.3 us
    pallas_call x5, Pallas kernels, put(): pl.pallas_call(functools.partial(put_kernel, owners, chunk, chunks, count...  22 us
    pallas_call x8, Pallas kernels, place(): pl.pallas_call(place_kernel, grid=(points // tile,), in_specs=[pl.BlockSp...  22 us
    unnamed x99, local copies, waits for them, and re-layouts  17.5 us
  transfers between devices with their start and end apart: 74, of which 28 were waited for; matrix products, arithmetic and copies ran while one was open for 4% of the time, Pallas kernels for 44%

profile of v4, /device:TPU:0, one launch (start us, length us, event | category | flops | bytes accessed | tf_op | source)
XLA Modules:
  0.0 589.4 jit_solution(12099165938110382935)
XLA Ops:
  9.8 45.5 %encode_own.2.refs_4_ = f32[2,3,16,1024]{3,2,1,0:T(8,128)} custom-call(s32[4]{0:T(128)} %pad_add_fusion.refs_0_.at_ref, f32[64,128,512]{2,1,0:T(8,128)} %refs_8_.7, f32[512,2048]{1,0:T(8,128)} %refs_2_.6, f32[128,2048]{1,0:T(8,128)} %refs_2_.7), custom_call_target="tpu_custom_call" | custom-call | flops 1610612736 | bytes 786432 | tf_op jit(solution)/shard_map/encode_own/pallas_call | solution.py:46
  57.2 18.2 %encode_own.3.refs_3_ = f32[2,1,16,1024]{3,2,1,0:T(8,128)} custom-call(s32[4]{0:T(128)} %pad_add_fusion.refs_0_.at_ref, f32[64,128,512]{2,1,0:T(8,128)} %refs_8_.7, f32[512,2048]{1,0:T(8,128)} %refs_2_.6, f32[128,2048]{1,0:T(8,128)} %refs_2_.7, f32[2,3,16,1024]{3,2,1,0:T(8,128)} %encode_own.2.refs_4_, ...), custom_call_target="tpu_custom_call" | custom-call | flops 536870912 | bytes 262144 | tf_op jit(solution)/shard_map/encode_own/pallas_call | solution.py:46
  79.3 7.3 %collective-permute-done.3 = f32[2,1,2,16,1024]{4,3,0,2,1:T(8,128)S(1)} collective-permute-done((f32[2,1,2,16,1024]{4,3,0,2,1:T(8,128)S(1)}, f32[2,1,2,16,1024]{4,3,0,2,1:T(8,128)S(1)}, u32[]{:S(2)}, u32[]{:S(2)}) %collective-permute-start.3) | collective-permute-done | bytes 262176 | tf_op jit(solution)/shard_map/ppermute | solution.py:362
  96.9 11.1 %collective-permute-done.4 = f32[4,1,1,16,1024]{4,3,0,2,1:T(8,128)S(1)} collective-permute-done((f32[4,1,1,16,1024]{4,3,0,2,1:T(8,128)S(1)}, f32[4,1,1,16,1024]{4,3,0,2,1:T(8,128)S(1)}, u32[]{:S(2)}, u32[]{:S(2)}) %collective-permute-start.4) | collective-permute-done | bytes 262176 | tf_op jit(solution)/shard_map/ppermute | solution.py:362
  142.6 6.1 %collective-permute-done.10 = f32[2,2,16,1024]{3,2,1,0:T(8,128)S(1)} collective-permute-done((f32[2,2,16,1024]{3,2,1,0:T(8,128)}, f32[2,2,16,1024]{3,2,1,0:T(8,128)S(1)}, u32[]{:S(2)}, u32[]{:S(2)}) %collective-permute-start.10) | collective-permute-done | bytes 262176 | tf_op jit(solution)/shard_map/ppermute | solution.py:362
  167.4 17.2 %interact.2 = f32[4,4,16,512]{3,2,1,0:T(8,128)} custom-call(s32[4]{0:T(128)} %pad_add_fusion.refs_0_.at_ref, f32[8,2,16,1024]{3,2,1,0:T(8,128)} %pad_maximum_fusion.refs_1_, f32[2048,4096]{1,0:T(8,128)} %refs_2_.9, f32[2,1,16,1024]{3,2,1,0:T(8,128)} %encode_own.3.refs_3_, f32[256,2048]{1,0:T(8,128)} %collective-permute-done.refs_5_.c_ref.refs_4_, ...), custom_call_target="tpu_custom_call" | custom-call | flops 201326592 | bytes 2097152 | tf_op jit(solution)/shard_map/interact/pallas_call | solution.py:46
  228.9 31.1 %decode.7.refs_7_ = f32[16,128,256]{2,1,0:T(8,128)} custom-call(s32[4]{0:T(128)} %pad_add_fusion.refs_0_.at_ref, f32[4,4,16,512]{3,2,1,0:T(8,128)} %pad_maximum_fusion.5.refs_1_, bf16[8,256,2048]{2,1,0:T(8,128)(2,1)} %get-tuple-element.70.refs_2_, bf16[8,256,2048]{2,1,0:T(8,128)(2,1)} %get-tuple-element.71.refs_3_, ...), custom_call_target="tpu_custom_call" | custom-call | flops 25769803776 | bytes 12582912 | tf_op jit(solution)/shard_map/decode/pallas_call | solution.py:46
  260.9 33.2 %decode.8.refs_1_.refs_8_.refs_7_ = f32[16,128,256]{2,1,0:T(8,128)} custom-call(s32[4]{0:T(128)} %pad_add_fusion.refs_0_.at_ref, f32[4,4,16,512]{3,2,1,0:T(8,128)} %pad_maximum_fusion.4.refs_1_, bf16[8,256,2048]{2,1,0:T(8,128)(2,1)} %get-tuple-element.70.refs_2_, bf16[8,256,2048]{2,1,0:T(8,128)(2,1)} %get-tuple-element.71.refs_3_, ...), custom_call_target="tpu_custom_call" | custom-call | flops 25769803776 | bytes 12582912 | tf_op jit(solution)/shard_map/decode/pallas_call | solution.py:46
  294.1 32.1 %encode_all.2.refs_5_ = f32[4,2,16,1024]{3,2,1,0:T(8,128)} custom-call(s32[4]{0:T(128)} %pad_add_fusion.refs_0_.at_ref, f32[16,128,256]{2,1,0:T(8,128)} %decode.8.refs_1_.refs_8_.refs_7_, bf16[8,256,2048]{2,1,0:T(8,128)(2,1)} %get-tuple-element.70.refs_2_, bf16[8,256,2048]{2,1,0:T(8,128)(2,1)} %get-tuple-element.71.refs_3_, ...), custom_call_target="tpu_custom_call" | custom-call | flops 25769803776 | bytes 12582912 | tf_op jit(solution)/shard_map/encode_all/pallas_call | solution.py:46
  326.7 32.3 %encode_all.3 = f32[4,2,16,1024]{3,2,1,0:T(8,128)} custom-call(s32[4]{0:T(128)} %pad_add_fusion.refs_0_.at_ref, f32[16,128,256]{2,1,0:T(8,128)} %decode.8.refs_1_.refs_8_.refs_7_, bf16[8,256,2048]{2,1,0:T(8,128)(2,1)} %get-tuple-element.70.refs_2_, bf16[8,256,2048]{2,1,0:T(8,128)(2,1)} %get-tuple-element.71.refs_3_, ...), custom_call_target="tpu_custom_call" | custom-call | flops 25769803776 | bytes 12582912 | tf_op jit(solution)/shard_map/encode_all/pallas_call | solution.py:46
  360.2 7.8 %collective-permute-done.32 = f32[2,2,16,1024]{3,2,1,0:T(8,128)S(1)} collective-permute-done((f32[2,2,16,1024]{3,2,1,0:T(8,128)S(1)}, f32[2,2,16,1024]{3,2,1,0:T(8,128)S(1)}, u32[]{:S(2)}, u32[]{:S(2)}) %collective-permute-start.32) | collective-permute-done | bytes 262176 | tf_op jit(solution)/shard_map/ppermute | solution.py:362
  380.7 6.0 %collective-permute-done.35 = f32[2,2,16,1024]{3,2,1,0:T(8,128)S(1)} collective-permute-done((f32[2,2,16,1024]{3,2,1,0:T(8,128)S(1)}, f32[2,2,16,1024]{3,2,1,0:T(8,128)S(1)}, u32[]{:S(2)}, u32[]{:S(2)}) %collective-permute-start.35) | collective-permute-done | bytes 262176 | tf_op jit(solution)/shard_map/ppermute | solution.py:362
  389.8 17.2 %interact.3 = f32[4,4,16,512]{3,2,1,0:T(8,128)} custom-call(s32[4]{0:T(128)} %pad_add_fusion.refs_0_.at_ref, f32[8,2,16,1024]{3,2,1,0:T(8,128)} %pad_maximum_fusion.1.refs_1_, f32[2048,4096]{1,0:T(8,128)} %refs_2_.9), custom_call_target="tpu_custom_call" | custom-call | flops 201326592 | bytes 2097152 | tf_op jit(solution)/shard_map/interact/pallas_call | solution.py:46
  410.2 8.0 %collective-permute-done.38 = f32[4,2,1,16,512]{4,3,1,0,2:T(8,128)S(1)} collective-permute-done((f32[4,2,1,16,512]{4,3,1,0,2:T(8,128)S(1)}, f32[4,2,1,16,512]{4,3,1,0,2:T(8,128)S(1)}, u32[]{:S(2)}, u32[]{:S(2)}) %collective-permute-start.38) | collective-permute-done | bytes 262176 | tf_op jit(solution)/shard_map/ppermute | solution.py:362
  418.3 7.5 %collective-permute-done.39 = f32[2,4,16,512]{3,2,1,0:T(8,128)S(1)} collective-permute-done((f32[2,4,16,512]{3,2,1,0:T(8,128)S(1)}, f32[2,4,16,512]{3,2,1,0:T(8,128)S(1)}, u32[]{:S(2)}, u32[]{:S(2)}) %collective-permute-start.39) | collective-permute-done | bytes 262176 | tf_op jit(solution)/shard_map/ppermute | solution.py:362
  427.1 6.3 %collective-permute-done.40 = f32[1,4,16,512]{3,2,1,0:T(8,128)S(1)} collective-permute-done((f32[1,4,16,512]{3,2,1,0:T(8,128)S(1)}, f32[1,4,16,512]{3,2,1,0:T(8,128)S(1)}, u32[]{:S(2)}, u32[]{:S(2)}) %collective-permute-start.40) | collective-permute-done | bytes 131104 | tf_op jit(solution)/shard_map/ppermute | solution.py:362
  433.5 7.9 %collective-permute-done.41 = f32[1,4,16,512]{3,2,1,0:T(8,128)S(1)} collective-permute-done((f32[1,4,16,512]{3,2,1,0:T(8,128)S(1)}, f32[1,4,16,512]{3,2,1,0:T(8,128)S(1)}, u32[]{:S(2)}, u32[]{:S(2)}) %collective-permute-start.41) | collective-permute-done | bytes 131104 | tf_op jit(solution)/shard_map/ppermute | solution.py:362
  443.6 6.0 %collective-permute-done.42 = f32[2,4,16,512]{3,2,1,0:T(8,128)S(1)} collective-permute-done((f32[2,4,16,512]{3,2,1,0:T(8,128)S(1)}, f32[2,4,16,512]{3,2,1,0:T(8,128)S(1)}, u32[]{:S(2)}, u32[]{:S(2)}) %collective-permute-start.42) | collective-permute-done | bytes 262176 | tf_op jit(solution)/shard_map/ppermute | solution.py:362
  451.9 10.9 %decode.9.refs_7_ = f32[4,128,256]{2,1,0:T(8,128)} custom-call(s32[4]{0:T(128)} %pad_add_fusion.refs_0_.at_ref, f32[4,4,16,512]{3,2,1,0:T(8,128)} %pad_maximum_fusion.7.refs_1_, bf16[8,256,2048]{2,1,0:T(8,128)(2,1)} %get-tuple-element.70.refs_2_, bf16[8,256,2048]{2,1,0:T(8,128)(2,1)} %get-tuple-element.71.refs_3_, ...), custom_call_target="tpu_custom_call" | custom-call | flops 6442450944 | bytes 12582912 | tf_op jit(solution)/shard_map/decode/pallas_call | solution.py:46
  463.7 11.6 %decode.10.refs_9_.refs_12_.refs_0_ = f32[4,128,256]{2,1,0:T(8,128)} custom-call(s32[4]{0:T(128)} %pad_add_fusion.refs_0_.at_ref, f32[4,4,16,512]{3,2,1,0:T(8,128)} %pad_maximum_fusion.8.refs_1_, bf16[8,256,2048]{2,1,0:T(8,128)(2,1)} %get-tuple-element.70.refs_2_, bf16[8,256,2048]{2,1,0:T(8,128)(2,1)} %get-tuple-element.71.refs_3_, ...), custom_call_target="tpu_custom_call" | custom-call | flops 6442450944 | bytes 12582912 | tf_op jit(solution)/shard_map/decode/pallas_call | solution.py:46
  477.4 19.3 %decode.11.refs_9_.refs_0_ = f32[4,128,256]{2,1,0:T(8,128)} custom-call(s32[4]{0:T(128)} %pad_add_fusion.refs_0_.at_ref, f32[4,8,16,512]{3,2,1,0:T(8,128)} %maximum_maximum_fusion.refs_1_, bf16[8,256,2048]{2,1,0:T(8,128)(2,1)} %get-tuple-element.70.refs_2_, bf16[8,256,2048]{2,1,0:T(8,128)(2,1)} %get-tuple-element.71.refs_3_, ...), custom_call_target="tpu_custom_call" | custom-call | flops 12884901888 | bytes 25165824 | tf_op jit(solution)/shard_map/decode/pallas_call | solution.py:46
  500.8 19.0 %decode.12.refs_9_.refs_0_ = f32[4,128,256]{2,1,0:T(8,128)} custom-call(s32[4]{0:T(128)} %pad_add_fusion.refs_0_.at_ref, f32[4,8,16,512]{3,2,1,0:T(8,128)} %maximum_maximum_fusion.refs_1_, bf16[8,256,2048]{2,1,0:T(8,128)(2,1)} %get-tuple-element.70.refs_2_, bf16[8,256,2048]{2,1,0:T(8,128)(2,1)} %get-tuple-element.71.refs_3_, ...), custom_call_target="tpu_custom_call" | custom-call | flops 12884901888 | bytes 25165824 | tf_op jit(solution)/shard_map/decode/pallas_call | solution.py:46
  523.6 19.0 %decode.13.refs_0_ = f32[4,128,256]{2,1,0:T(8,128)} custom-call(s32[4]{0:T(128)} %pad_add_fusion.refs_0_.at_ref, f32[4,8,16,512]{3,2,1,0:T(8,128)} %maximum_maximum_fusion.refs_1_, bf16[8,256,2048]{2,1,0:T(8,128)(2,1)} %get-tuple-element.70.refs_2_, bf16[8,256,2048]{2,1,0:T(8,128)(2,1)} %get-tuple-element.71.refs_3_, ...), custom_call_target="tpu_custom_call" | custom-call | flops 12884901888 | bytes 25165824 | tf_op jit(solution)/shard_map/decode/pallas_call | solution.py:46
  546.7 10.2 %collective-permute-done.61.refs_1_ = f32[4,128,256]{2,1,0:T(8,128)S(1)} collective-permute-done((f32[4,128,256]{2,1,0:T(8,128)}, f32[4,128,256]{2,1,0:T(8,128)S(1)}, u32[]{:S(2)}, u32[]{:S(2)}) %collective-permute-start.61) | collective-permute-done | bytes 524320 | tf_op jit(solution)/shard_map/ppermute | solution.py:362
  (301 shorter events, 197.5 us)
Async XLA Ops:
  4.7 50.5 %collective-permute-start = (f32[256,2048]{1,0:T(8,128)}, f32[256,2048]{1,0:T(8,128)}, u32[]{:S(2)}, u32[]{:S(2)}) collective-permute-start(f32[256,2048]{1,0:T(8,128)} %get-tuple-element.96), channel_id=1, source_target_pairs={{0,8},{4,12},{8,0},{12,4},{16,24},{20,28},{24,16},{28,20},{1,9},{5... | collective-permute-start | bytes 6291464 | tf_op jit(solution)/shard_map/ppermute | solution.py:362
  7.7 48.2 %collective-permute-start.1 = (f32[256,2048]{1,0:T(8,128)}, f32[256,2048]{1,0:T(8,128)S(1)}, u32[]{:S(2)}, u32[]{:S(2)}) collective-permute-start(f32[256,2048]{1,0:T(8,128)} %get-tuple-element.95.c_ref), channel_id=1, source_target_pairs={{0,16},{4,20},{8,24},{12,28},{16,0},{20,4},{24,8},{28,12},{1,17},{... | collective-permute-start | bytes 6291464 | tf_op jit(solution)/shard_map/ppermute | solution.py:362
  55.3 53.6 %collective-permute-start.5 = (f32[256,2048]{1,0:T(8,128)}, f32[256,2048]{1,0:T(8,128)S(1)}, u32[]{:S(2)}, u32[]{:S(2)}) collective-permute-start(f32[256,2048]{1,0:T(8,128)} %collective-permute-done.refs_5_.c_ref.refs_4_), channel_id=1, source_target_pairs={{0,16},{4,20},{8,24},{12,28},{16,0},{20,4},{24,8},{28,12},{1,17},{... | collective-permute-start | bytes 6291464 | tf_op jit(solution)/shard_map/ppermute | solution.py:362
  88.3 62.2 %collective-permute-start.24 = (f32[256,2048]{1,0:T(8,128)}, f32[256,2048]{1,0:T(8,128)}, u32[]{:S(2)}, u32[]{:S(2)}) collective-permute-start(f32[256,2048]{1,0:T(8,128)} %get-tuple-element.95.c_ref), channel_id=1, source_target_pairs={{0,4},{4,0},{8,12},{12,8},{16,20},{20,16},{24,28},{28,24},{1,5},{5... | collective-permute-start | bytes 6291464 | tf_op jit(solution)/shard_map/ppermute | solution.py:362
  91.0 68.9 %collective-permute-start.22 = (f32[256,2048]{1,0:T(8,128)S(1)}, f32[256,2048]{1,0:T(8,128)}, u32[]{:S(2)}, u32[]{:S(2)}) collective-permute-start(f32[256,2048]{1,0:T(8,128)S(1)} %copy-done.1), channel_id=1, source_target_pairs={{0,4},{4,0},{8,12},{12,8},{16,20},{20,16},{24,28},{28,24},{1,5},{5... | collective-permute-start | bytes 6291464 | tf_op jit(solution)/shard_map/ppermute | solution.py:362
  91.5 65.7 %collective-permute-start.23 = (f32[256,2048]{1,0:T(8,128)}, f32[256,2048]{1,0:T(8,128)}, u32[]{:S(2)}, u32[]{:S(2)}) collective-permute-start(f32[256,2048]{1,0:T(8,128)} %collective-permute-done.refs_5_.c_ref.refs_4_), channel_id=1, source_target_pairs={{0,4},{4,0},{8,12},{12,8},{16,20},{20,16},{24,28},{28,24},{1,5},{5... | collective-permute-start | bytes 6291464 | tf_op jit(solution)/shard_map/ppermute | solution.py:362
  116.1 23.3 %collective-permute-start.9 = (f32[128,2048]{1,0:T(8,128)}, f32[128,2048]{1,0:T(8,128)S(1)}, u32[]{:S(2)}, u32[]{:S(2)}) collective-permute-start(f32[128,2048]{1,0:T(8,128)} %get-tuple-element.59), channel_id=1, source_target_pairs={{0,16},{4,20},{8,24},{12,28},{16,0},{20,4},{24,8},{28,12},{1,17},{... | collective-permute-start | bytes 3145736 | tf_op jit(solution)/shard_map/ppermute | solution.py:362
  135.8 28.9 %collective-permute-start.27 = (f32[128,2048]{1,0:T(8,128)}, f32[128,2048]{1,0:T(8,128)S(1)}, u32[]{:S(2)}, u32[]{:S(2)}) collective-permute-start(f32[128,2048]{1,0:T(8,128)} %get-tuple-element.59), channel_id=1, source_target_pairs={{0,8},{4,12},{8,0},{12,4},{16,24},{20,28},{24,16},{28,20},{1,9},{5... | collective-permute-start | bytes 3145736 | tf_op jit(solution)/shard_map/ppermute | solution.py:362
  148.7 37.0 %collective-permute-start.25 = (f32[128,2048]{1,0:T(8,128)}, f32[128,2048]{1,0:T(8,128)}, u32[]{:S(2)}, u32[]{:S(2)}) collective-permute-start(f32[128,2048]{1,0:T(8,128)} %get-tuple-element.59), channel_id=1, source_target_pairs={{0,4},{4,0},{8,12},{12,8},{16,20},{20,16},{24,28},{28,24},{1,5},{5... | collective-permute-start | bytes 3145736 | tf_op jit(solution)/shard_map/ppermute | solution.py:362
  157.2 33.1 %collective-permute-start.21 = (f32[256,2048]{1,0:T(8,128)S(1)}, f32[256,2048]{1,0:T(8,128)}, u32[]{:S(2)}, u32[]{:S(2)}) collective-permute-start(f32[256,2048]{1,0:T(8,128)S(1)} %copy-done.3), channel_id=1, source_target_pairs={{0,4},{4,0},{8,12},{12,8},{16,20},{20,16},{24,28},{28,24},{1,5},{5... | collective-permute-start | bytes 6291464 | tf_op jit(solution)/shard_map/ppermute | solution.py:362
  164.3 33.3 %collective-permute-start.26 = (f32[128,2048]{1,0:T(8,128)S(1)}, f32[128,2048]{1,0:T(8,128)S(1)}, u32[]{:S(2)}, u32[]{:S(2)}) collective-permute-start(f32[128,2048]{1,0:T(8,128)S(1)} %copy-done.6), channel_id=1, source_target_pairs={{0,4},{4,0},{8,12},{12,8},{16,20},{20,16},{24,28},{28,24},{1,5},{5... | collective-permute-start | bytes 3145736 | tf_op jit(solution)/shard_map/ppermute | solution.py:362
  164.8 43.8 %collective-permute-start.29 = (f32[128,2048]{1,0:T(8,128)S(1)}, f32[128,2048]{1,0:T(8,128)S(1)}, u32[]{:S(2)}, u32[]{:S(2)}) collective-permute-start(f32[128,2048]{1,0:T(8,128)S(1)} %copy-done.6), channel_id=1, source_target_pairs={{0,8},{4,12},{8,0},{12,4},{16,24},{20,28},{24,16},{28,20},{1,9},{5... | collective-permute-start | bytes 3145736 | tf_op jit(solution)/shard_map/ppermute | solution.py:362
  165.3 48.2 %collective-permute-start.28 = (f32[128,2048]{1,0:T(8,128)S(1)}, f32[128,2048]{1,0:T(8,128)S(1)}, u32[]{:S(2)}, u32[]{:S(2)}) collective-permute-start(f32[128,2048]{1,0:T(8,128)S(1)} %collective-permute-done.27), channel_id=1, source_target_pairs={{0,4},{4,0},{8,12},{12,8},{16,20},{20,16},{24,28},{28,24},{1,5},{5... | collective-permute-start | bytes 3145736 | tf_op jit(solution)/shard_map/ppermute | solution.py:362
  220.2 39.8 %collective-permute-start.16 = (f32[1,4,16,512]{3,2,1,0:T(8,128)S(1)}, f32[1,4,16,512]{3,2,1,0:T(8,128)S(1)}, u32[]{:S(2)}, u32[]{:S(2)}) collective-permute-start(f32[1,4,16,512]{3,2,1,0:T(8,128)S(1)} %fusion.16), channel_id=1, source_target_pairs={{0,8},{4,12},{8,0},{12,4},{16,24},{20,28},{24,16},{28,20},{1,9},{5... | collective-permute-start | bytes 393224 | tf_op jit(solution)/shard_map/ppermute | solution.py:362
  221.7 38.3 %collective-permute-start.20 = (f32[1,4,16,512]{3,2,1,0:T(8,128)S(1)}, f32[1,4,16,512]{3,2,1,0:T(8,128)S(1)}, u32[]{:S(2)}, u32[]{:S(2)}) collective-permute-start(f32[1,4,16,512]{3,2,1,0:T(8,128)S(1)} %collective-permute-done.17), channel_id=1, source_target_pairs={{0,8},{4,12},{8,0},{12,4},{16,24},{20,28},{24,16},{28,20},{1,9},{5... | collective-permute-start | bytes 393224 | tf_op jit(solution)/shard_map/ppermute | solution.py:362
  225.4 34.5 %collective-permute-start.19 = (f32[2,4,16,512]{3,2,1,0:T(8,128)S(1)}, f32[2,4,16,512]{3,2,1,0:T(8,128)S(1)}, u32[]{:S(2)}, u32[]{:S(2)}) collective-permute-start(f32[2,4,16,512]{3,2,1,0:T(8,128)S(1)} %collective-permute-done.18), channel_id=1, source_target_pairs={{0,8},{4,12},{8,0},{12,4},{16,24},{20,28},{24,16},{28,20},{1,9},{5... | collective-permute-start | bytes 786440 | tf_op jit(solution)/shard_map/ppermute | solution.py:362
  326.2 32.8 %collective-permute-start.31 = (f32[4,2,16,1024]{3,2,1,0:T(8,128)}, f32[4,2,16,1024]{3,2,1,0:T(8,128)S(1)}, u32[]{:S(2)}, u32[]{:S(2)}) collective-permute-start(f32[4,2,16,1024]{3,2,1,0:T(8,128)} %encode_all.2.refs_5_), channel_id=1, source_target_pairs={{0,8},{4,12},{8,0},{12,4},{16,24},{20,28},{24,16},{28,20},{1,9},{5... | collective-permute-start | bytes 1572872 | tf_op jit(solution)/shard_map/ppermute | solution.py:362
  475.4 24.4 %collective-permute-start.46 = (f32[4,128,256]{2,1,0:T(8,128)}, f32[4,128,256]{2,1,0:T(8,128)S(1)}, u32[]{:S(2)}, u32[]{:S(2)}) collective-permute-start(f32[4,128,256]{2,1,0:T(8,128)} %decode.10.refs_9_.refs_12_.refs_0_), channel_id=1, source_target_pairs={{0,16},{4,20},{8,24},{12,28},{16,0},{20,4},{24,8},{28,12},{1,17},{... | collective-permute-start | bytes 1572872 | tf_op jit(solution)/shard_map/ppermute | solution.py:362
  475.9 23.8 %collective-permute-start.47 = (f32[4,128,256]{2,1,0:T(8,128)}, f32[4,128,256]{2,1,0:T(8,128)S(1)}, u32[]{:S(2)}, u32[]{:S(2)}) collective-permute-start(f32[4,128,256]{2,1,0:T(8,128)} %decode.10.refs_9_.refs_12_.refs_0_), channel_id=1, source_target_pairs={{0,8},{4,12},{8,0},{12,4},{16,24},{20,28},{24,16},{28,20},{1,9},{5... | collective-permute-start | bytes 1572872 | tf_op jit(solution)/shard_map/ppermute | solution.py:362
  496.7 23.9 %collective-permute-start.48 = (f32[4,128,256]{2,1,0:T(8,128)}, f32[4,128,256]{2,1,0:T(8,128)S(1)}, u32[]{:S(2)}, u32[]{:S(2)}) collective-permute-start(f32[4,128,256]{2,1,0:T(8,128)} %decode.11.refs_9_.refs_0_), channel_id=1, source_target_pairs={{0,16},{4,20},{8,24},{12,28},{16,0},{20,4},{24,8},{28,12},{1,17},{... | collective-permute-start | bytes 1572872 | tf_op jit(solution)/shard_map/ppermute | solution.py:362
  498.3 23.3 %collective-permute-start.49 = (f32[4,128,256]{2,1,0:T(8,128)}, f32[4,128,256]{2,1,0:T(8,128)S(1)}, u32[]{:S(2)}, u32[]{:S(2)}) collective-permute-start(f32[4,128,256]{2,1,0:T(8,128)} %decode.11.refs_9_.refs_0_), channel_id=1, source_target_pairs={{0,8},{4,12},{8,0},{12,4},{16,24},{20,28},{24,16},{28,20},{1,9},{5... | collective-permute-start | bytes 1572872 | tf_op jit(solution)/shard_map/ppermute | solution.py:362
  519.9 26.2 %collective-permute-start.68 = (f32[4,128,256]{2,1,0:T(8,128)}, f32[4,128,256]{2,1,0:T(8,128)S(1)}, u32[]{:S(2)}, u32[]{:S(2)}) collective-permute-start(f32[4,128,256]{2,1,0:T(8,128)} %decode.12.refs_9_.refs_0_), channel_id=1, source_target_pairs={{0,8},{4,12},{8,0},{12,4},{16,24},{20,28},{24,16},{28,20},{1,9},{5... | collective-permute-start | bytes 1572872 | tf_op jit(solution)/shard_map/ppermute | solution.py:362
  520.6 26.0 %collective-permute-start.69 = (f32[4,128,256]{2,1,0:T(8,128)}, f32[4,128,256]{2,1,0:T(8,128)S(1)}, u32[]{:S(2)}, u32[]{:S(2)}) collective-permute-start(f32[4,128,256]{2,1,0:T(8,128)} %decode.12.refs_9_.refs_0_), channel_id=1, source_target_pairs={{0,16},{4,20},{8,24},{12,28},{16,0},{20,4},{24,8},{28,12},{1,17},{... | collective-permute-start | bytes 1572872 | tf_op jit(solution)/shard_map/ppermute | solution.py:362
  522.2 23.9 %collective-permute-start.58 = (f32[4,128,256]{2,1,0:T(8,128)S(1)}, f32[4,128,256]{2,1,0:T(8,128)S(1)}, u32[]{:S(2)}, u32[]{:S(2)}) collective-permute-start(f32[4,128,256]{2,1,0:T(8,128)S(1)} %collective-permute-done.48.refs_10_.refs_4_), channel_id=1, source_target_pairs={{0,8},{4,12},{8,0},{12,4},{16,24},{20,28},{24,16},{28,20},{1,9},{5... | collective-permute-start | bytes 1572872 | tf_op jit(solution)/shard_map/ppermute | solution.py:362
  (94 other events, 928.5 us)
